TPU v7x, 128 devices: a whole 4x4x4 slice. The times are simulated.
128 devices in a mesh: blk: 32 (over y, z, core), span: 4 (over x).
Axes of the slice: x: 4, y: 4, z: 4, core: 2. Of those that a mesh axis runs over, the one named last changes fastest.
Arguments:
- disp: float32 [3, 24, 64, 4096], P(None, None, 'span', 'blk'), may hold values from -6 to 6
- velocity: float32 [3, 24, 64, 4096], P(None, None, 'span', 'blk'), may hold values from -3 to 3
- modulus: float32 [24, 64, 4096], P(None, 'span', 'blk'), may hold values from 0.5 to 4
- guess_circ: float32 [32, 2, 6, 3, 24, 64], P('blk', None, None, None, None, 'span'), may hold values from -6 to 6
- guess_height: float32 [4, 2, 6, 3, 24, 4096], P('span', None, None, None, None, 'blk'), may hold values from -6 to 6
- pair_match: int32 [32, 4, 384], P('blk', 'span'), may hold values from 0 to 383, each once within a row
- patch_owner: int32 [32, 4, 384], P('blk', 'span'), may hold values from 0 to 4095
Outputs:
- disp_end: float32 [3, 24, 64, 4096], P(None, None, 'span', 'blk')
- circ_next: float32 [32, 2, 6, 3, 24, 64], P('blk', None, None, None, None, 'span')
- height_next: float32 [4, 2, 6, 3, 24, 4096], P('span', None, None, None, None, 'blk')
- patch_load: float32 [3, 4096], P(None, ('blk', 'span'))
Inputs may be any that keep to these rules, and one draw needn't show every extreme that they name: `pair_match`: each device's block of 384 entries is a permutation.
All inputs are finite; a program needn't handle non-finite values.
Results may differ from a plain program's by a relative error of at most 0.0003.
Values sent between devices are 32-bit elements; how exact they have to be, the bound alone decides.
No kernel may reach another device: no remote copies, remote signals or barrier semaphores. Data moves between devices by JAX's collectives and lax.ppermute only.
A program may use at most 128 MiB of HBM per device.

v0:
```python
import jax
import jax.numpy as jnp
from jax import lax
from jax.sharding import PartitionSpec as P

STEPS = 6
PATCH_DEV = 32


time_step = 0.2


def with_halo(cells, sides, width, closed):
    for axis, dim in sides:
        count = lax.axis_size(axis)
        ends = count if closed else count - 1
        head = lax.slice_in_dim(cells, 0, width, axis=dim)
        tail = lax.slice_in_dim(cells, cells.shape[dim] - width, cells.shape[dim], axis=dim)
        cells = jnp.concatenate(
            [
                lax.ppermute(tail, axis, [(i, (i + 1) % count) for i in range(ends)]),
                cells,
                lax.ppermute(head, axis, [((i + 1) % count, i) for i in range(ends)]),
            ],
            axis=dim,
        )
    return cells


def interior(current, faces):
    along_k, along_h, along_a = faces
    diff = along_k * (current[:, 1:] - current[:, :-1])
    total = jnp.pad(diff, ((0, 0), (0, 1), (0, 0), (0, 0))) - jnp.pad(
        diff, ((0, 0), (1, 0), (0, 0), (0, 0))
    )
    diff = along_h * (current[:, :, 1:] - current[:, :, :-1])
    total = (
        total
        + jnp.pad(diff, ((0, 0), (0, 0), (0, 1), (0, 0)))
        - jnp.pad(diff, ((0, 0), (0, 0), (1, 0), (0, 0)))
    )
    diff = along_a * (current[:, :, :, 1:] - current[:, :, :, :-1])
    total = (
        total
        + jnp.pad(diff, ((0, 0), (0, 0), (0, 0), (0, 1)))
        - jnp.pad(diff, ((0, 0), (0, 0), (0, 0), (1, 0)))
    )
    return total


def subdomain(start, speed, moduli, g_west, g_east, g_south, g_north):
    faces = (
        0.5 * (moduli[1:] + moduli[:-1]),
        0.5 * (moduli[:, 1:] + moduli[:, :-1]),
        0.5 * (moduli[:, :, 1:] + moduli[:, :, :-1]),
    )
    imp_west = jnp.sqrt(moduli[:, :, 0])
    imp_east = jnp.sqrt(moduli[:, :, -1])
    imp_south = jnp.sqrt(moduli[:, 0, :])
    imp_north = jnp.sqrt(moduli[:, -1, :])
    older = start - time_step * speed
    current = start
    records = [[], [], [], [], [], [], [], []]
    for step in range(STEPS):
        rate_w = imp_west * ((current[:, :, :, 0] - older[:, :, :, 0]) / time_step)
        rate_e = imp_east * ((current[:, :, :, -1] - older[:, :, :, -1]) / time_step)
        rate_s = imp_south * ((current[:, :, 0, :] - older[:, :, 0, :]) / time_step)
        rate_n = imp_north * ((current[:, :, -1, :] - older[:, :, -1, :]) / time_step)
        phi_w = g_west[step] - rate_w
        phi_e = g_east[step] - rate_e
        phi_s = g_south[step] - rate_s
        phi_n = g_north[step] - rate_n
        total = interior(current, faces)
        total = total.at[:, :, :, 0].add(phi_w).at[:, :, :, -1].add(phi_e)
        total = total.at[:, :, 0, :].add(phi_s).at[:, :, -1, :].add(phi_n)
        following = 2.0 * current - older + time_step * time_step * total
        older, current = (current, following)
        for slot, value in enumerate((phi_w, rate_w, phi_e, rate_e, phi_s, rate_s, phi_n, rate_n)):
            records[slot].append(value)
    stacked = [jnp.stack(item) for item in records]
    load = jnp.sum(stacked[2], axis=0)
    return (current,) + tuple(stacked) + (load,)


def exchange_faces(results, match):
    final, phi_w, rate_w, phi_e, rate_e, phi_s, rate_s, phi_n, rate_n, load = results
    layers, height = (phi_w.shape[2], phi_w.shape[3])
    flat = layers * height

    def flatten(values):
        return values.reshape(STEPS, 3, flat)

    def place(values):
        spread = flatten(values)
        return jnp.zeros_like(spread).at[:, :, match].set(spread)

    circ = jnp.stack(
        [jnp.stack([place(phi_w), place(rate_w)]), jnp.stack([flatten(phi_e), flatten(rate_e)])]
    )
    rising = jnp.stack([jnp.stack([phi_s, rate_s]), jnp.stack([phi_n, rate_n])])
    got_circ = with_halo(circ, (("blk", 0),), 1, True)
    got_rise = with_halo(rising, (("span", 0),), 1, False)
    from_left = got_circ[0, 1] - got_circ[0, 0]
    from_right = got_circ[3, 1] - got_circ[3, 0]
    below = got_rise[0, 1] - got_rise[0, 0]
    above = got_rise[3, 1] - got_rise[3, 0]
    shape = (STEPS, 3, layers, height)
    new_w = from_left[:, :, match].reshape(shape)
    new_e = from_right.reshape(shape)
    return (new_w, new_e, below, above)


def local(disp, velocity, modulus, guess_circ, guess_height, pair_match, patch_owner):
    match = pair_match[0, 0]
    owners = patch_owner[0, 0]
    data = (guess_circ[0, 0], guess_circ[0, 1], guess_height[0, 0], guess_height[0, 1])
    for sweep in range(2):
        results = subdomain(disp, velocity, modulus, *data)
        data = exchange_faces(results, match)
    final = results[0]
    load = results[9]
    patches_all = PATCH_DEV * lax.axis_size("blk") * lax.axis_size("span")
    partial_sums = jax.ops.segment_sum(load.reshape(3, -1).T, owners, num_segments=patches_all).T
    patch_load = lax.psum_scatter(partial_sums, ("blk", "span"), scatter_dimension=1, tiled=True)
    circ_next = jnp.stack([data[0], data[1]])[None]
    height_next = jnp.stack([data[2], data[3]])[None]
    return (final, circ_next, height_next, patch_load)


def solution(mesh):
    in_specs = (
        P(None, None, "span", "blk"),
        P(None, None, "span", "blk"),
        P(None, "span", "blk"),
        P("blk", None, None, None, None, "span"),
        P("span", None, None, None, None, "blk"),
        P("blk", "span", None),
        P("blk", "span", None),
    )
    out_specs = (
        P(None, None, "span", "blk"),
        P("blk", None, None, None, None, "span"),
        P("span", None, None, None, None, "blk"),
        P(None, ("blk", "span")),
    )
    return jax.shard_map(local, mesh=mesh, in_specs=in_specs, out_specs=out_specs, check_vma=False)
```

profile of v0, /device:TPU:0, one launch (start us, length us, event | category | flops | bytes accessed | tf_op | source)
XLA Modules:
  0.0 1419.1 jit_solution(10100931296347887770)
XLA Ops:
  41.5 8.6 pad_subtract_fusion.9
  66.7 6.3 multiply_add_fusion.7
  79.9 6.7 pad_subtract_fusion.8
  112.1 8.6 pad_subtract_fusion.7
  146.2 8.4 pad_subtract_fusion.6
  196.1 8.8 pad_subtract_fusion.5
  217.4 6.8 multiply_add_fusion.3
  309.1 5.5 copy.3143
  385.9 38.4 %scatter_fusion = f32[6,3,384]{0,1,2:T(4,128)} fusion(f32[6,3,384]{0,1,2:T(4,128)} %broadcast.1874.clone.1, s32[384]{0:T(512)S(1)} %fusion.69, f32[384,6,3]{1,2,0:T(4,128)} %copy.3158), kind=kCustom, calls=%fused_computation.2 | custom fusion | bytes 84480 | tf_op jit(solution)/shard_map/scatter | solution.py:95
  430.7 38.4 %scatter_fusion.1 = f32[6,3,384]{0,1,2:T(4,128)} fusion(f32[6,3,384]{0,1,2:T(4,128)} %broadcast.1874.clone, s32[384]{0:T(512)S(1)} %fusion.69, f32[384,6,3]{1,2,0:T(4,128)} %copy.3159), kind=kCustom, calls=%fused_computation.3 | custom fusion | bytes 84480 | tf_op jit(solution)/shard_map/scatter | solution.py:95
  472.6 6.1 collective-permute-start.1
  567.1 6.6 scatter-add.190
  577.0 6.8 scatter-add.191
  598.0 6.8 pad_subtract_fusion.4
  615.4 6.2 broadcast_multiply_fusion.3
  627.9 6.8 pad_subtract_fusion.3
  661.5 6.7 pad_subtract_fusion.2
  679.2 7.5 broadcast_multiply_fusion.2
  693.2 6.7 pad_subtract_fusion.1
  740.3 8.6 pad_subtract_fusion
  810.3 38.6 %scatter_fusion.2 = f32[6,3,384]{0,1,2:T(4,128)} fusion(f32[6,3,384]{0,1,2:T(4,128)} %broadcast.1874.clone.3, s32[384]{0:T(512)S(1)} %fusion.69, f32[384,6,3]{1,2,0:T(4,128)} %copy.3278), kind=kCustom, calls=%fused_computation.4 | custom fusion | bytes 84480 | tf_op jit(solution)/shard_map/scatter | solution.py:95
  853.3 38.6 %scatter_fusion.3 = f32[6,3,384]{0,1,2:T(4,128)} fusion(f32[6,3,384]{0,1,2:T(4,128)} %broadcast.1874.clone.2, s32[384]{0:T(512)S(1)} %fusion.69, f32[384,6,3]{1,2,0:T(4,128)} %copy.3279), kind=kCustom, calls=%fused_computation.5 | custom fusion | bytes 84480 | tf_op jit(solution)/shard_map/scatter | solution.py:95
  900.7 5.9 multiply_add_fusion
  914.7 493.0 %reduce-scatter.2.cloned.1.call-done = f32[3,32]{0,1:T(8,128)} async-done(((f32[3,4096]{0,1:T(8,128)}), f32[3,32]{0,1:T(8,128)}) %reduce-scatter.2.cloned.1.call-update) | async-done | bytes 400 | tf_op jit(solution)/shard_map/reduce_scatter | solution.py:124
  (687 shorter events, 622.1 us)
Async XLA Ops:
  7.2 1400.6 %reduce-scatter.2.cloned.1.call-start = ((), (), s32[]{:S(2)}) async-start(), calls=%async_computation.1 | async-start | bytes 2113536 | tf_op jit(solution)/shard_map/reduce_scatter | solution.py:124
  229.6 78.9 %copy-start.120 = (s32[1,1,384]{2,1,0:T(1,128)S(1)}, s32[1,1,384]{2,1,0:T(1,128)}, u32[]{:S(2)}) copy-start(s32[1,1,384]{2,1,0:T(1,128)} %param.100) | copy-start | bytes 4612
  258.1 244.3 %collective-permute-start.3 = (f32[1,2,6,3,24,128]{5,4,3,2,1,0:T(8,128)}, f32[1,2,6,3,24,128]{5,4,3,2,1,0:T(8,128)}, u32[]{:S(2)}, u32[]{:S(2)}) collective-permute-start(f32[1,2,6,3,24,128]{5,4,3,2,1,0:T(8,128)} %maximum_bitcast_fusion.1), channel_id=1, source_target_pairs={{1,0},{2,1},{3,2},{5,4},{6,5},{7,6},{9,8},{10,9},{11,10},{13,12},{... | collective-permute-start | bytes 1327112 | tf_op jit(solution)/shard_map/ppermute | solution.py:23
  267.1 41.4 %copy-start.116 = (f32[1,1,3,384]{3,0,2,1:T(1,128)}, f32[1,1,3,384]{3,0,2,1:T(1,128)S(1)}, u32[]{:S(2)}) copy-start(f32[1,1,3,384]{3,0,2,1:T(1,128)S(1)} %sub.1705) | copy-start | bytes 13828
  308.5 61.3 %collective-permute-start = (f32[1,2,6,3,384]{4,1,3,2,0:T(2,128)}, f32[1,2,6,3,384]{4,1,3,2,0:T(2,128)}, u32[]{:S(2)}, u32[]{:S(2)}) collective-permute-start(f32[1,2,6,3,384]{4,1,3,2,0:T(2,128)} %maximum_bitcast_fusion.6), channel_id=1, source_target_pairs={{0,4},{4,8},{8,12},{12,16},{16,20},{20,24},{24,28},{28,32},{32,36}... | collective-permute-start | bytes 165896 | tf_op jit(solution)/shard_map/ppermute | solution.py:21
  314.6 54.6 %copy-start.121 = (s32[1,1,384]{2,1,0:T(1,128)S(1)}, s32[1,1,384]{2,1,0:T(1,128)}, u32[]{:S(2)}) copy-start(s32[1,1,384]{2,1,0:T(1,128)} %param.101) | copy-start | bytes 4612
  315.3 50.3 %copy-start.100 = (f32[1,1,1,3,24,16]{4,5,3,2,1,0:T(8,128)S(1)}, f32[1,1,1,3,24,16]{4,5,3,2,1,0:T(8,128)}, u32[]{:S(2)}) copy-start(f32[1,1,1,3,24,16]{4,5,3,2,1,0:T(8,128)} %get-tuple-element.789) | copy-start | bytes 13828
  375.3 106.2 %copy-start.83 = (f32[3,24,16,1]{1,3,0,2:T(1,128)S(1)}, f32[3,24,16,1]{1,3,0,2:T(1,128)}, u32[]{:S(2)}) copy-start(f32[3,24,16,1]{1,3,0,2:T(1,128)} %get-tuple-element.719) | copy-start | bytes 13828
  472.6 24.7 %collective-permute-start.1 = (f32[1,2,6,3,384]{4,1,3,2,0:T(2,128)}, f32[1,2,6,3,384]{4,1,3,2,0:T(2,128)}, u32[]{:S(2)}, u32[]{:S(2)}) collective-permute-start(f32[1,2,6,3,384]{4,1,3,2,0:T(2,128)} %maximum_bitcast_fusion.7), channel_id=1, source_target_pairs={{4,0},{8,4},{12,8},{16,12},{20,16},{24,20},{28,24},{32,28},{36,32}... | collective-permute-start | bytes 165896 | tf_op jit(solution)/shard_map/ppermute | solution.py:23
  528.8 27.3 %collective-permute-start.2 = (f32[1,2,6,3,24,128]{5,4,3,2,1,0:T(8,128)}, f32[1,2,6,3,24,128]{5,4,3,2,1,0:T(8,128)}, u32[]{:S(2)}, u32[]{:S(2)}) collective-permute-start(f32[1,2,6,3,24,128]{5,4,3,2,1,0:T(8,128)} %maximum_bitcast_fusion), channel_id=1, source_target_pairs={{0,1},{1,2},{2,3},{4,5},{5,6},{6,7},{8,9},{9,10},{10,11},{12,13},{... | collective-permute-start | bytes 1327112 | tf_op jit(solution)/shard_map/ppermute | solution.py:21
  777.5 22.4 %copy-start.72 = (f32[1,3,24,128]{2,3,1,0:T(8,128)S(1)}, f32[1,3,24,128]{2,3,1,0:T(8,128)}, u32[]{:S(2)}) copy-start(f32[1,3,24,128]{2,3,1,0:T(8,128)} %get-tuple-element.744) | copy-start | bytes 110596
  777.5 22.5 %copy-start.71 = (f32[1,3,24,128]{2,3,1,0:T(8,128)S(1)}, f32[1,3,24,128]{2,3,1,0:T(8,128)}, u32[]{:S(2)}) copy-start(f32[1,3,24,128]{2,3,1,0:T(8,128)} %get-tuple-element.748) | copy-start | bytes 110596
  777.5 22.6 %copy-start.70 = (f32[1,3,24,128]{2,3,1,0:T(8,128)S(1)}, f32[1,3,24,128]{2,3,1,0:T(8,128)}, u32[]{:S(2)}) copy-start(f32[1,3,24,128]{2,3,1,0:T(8,128)} %get-tuple-element.723) | copy-start | bytes 110596
  777.6 22.7 %copy-start.75 = (f32[1,3,24,128]{2,3,1,0:T(8,128)S(1)}, f32[1,3,24,128]{2,3,1,0:T(8,128)}, u32[]{:S(2)}) copy-start(f32[1,3,24,128]{2,3,1,0:T(8,128)} %get-tuple-element.769) | copy-start | bytes 110596
  777.6 22.8 %copy-start.67 = (f32[6,3,24,128]{3,2,1,0:T(8,128)S(1)}, f32[6,3,24,128]{3,2,1,0:T(8,128)}, u32[]{:S(2)}) copy-start(f32[6,3,24,128]{3,2,1,0:T(8,128)} %copy.3490) | copy-start | bytes 663556
  777.6 22.8 %copy-start.74 = (f32[1,3,24,128]{2,3,1,0:T(8,128)S(1)}, f32[1,3,24,128]{2,3,1,0:T(8,128)}, u32[]{:S(2)}) copy-start(f32[1,3,24,128]{2,3,1,0:T(8,128)} %get-tuple-element.767) | copy-start | bytes 110596
  777.6 22.9 %copy-start.69 = (f32[1,3,24,128]{2,3,1,0:T(8,128)S(1)}, f32[1,3,24,128]{2,3,1,0:T(8,128)}, u32[]{:S(2)}) copy-start(f32[1,3,24,128]{2,3,1,0:T(8,128)} %get-tuple-element.745) | copy-start | bytes 110596
  796.2 612.9 %collective-permute-start.6 = (f32[1,2,6,3,24,128]{5,4,3,2,1,0:T(8,128)}, f32[1,2,6,3,24,128]{5,4,3,2,1,0:T(8,128)}, u32[]{:S(2)}, u32[]{:S(2)}) collective-permute-start(f32[1,2,6,3,24,128]{5,4,3,2,1,0:T(8,128)} %maximum_bitcast_fusion.3), channel_id=1, source_target_pairs={{0,1},{1,2},{2,3},{4,5},{5,6},{6,7},{8,9},{9,10},{10,11},{12,13},{... | collective-permute-start | bytes 1327112 | tf_op jit(solution)/shard_map/ppermute | solution.py:21
  800.2 50.0 %copy-start.114 = (f32[1,3,384]{2,0,1:T(1,128)S(1)}, f32[1,3,384]{2,0,1:T(1,128)}, u32[]{:S(2)}) copy-start(f32[1,3,384]{2,0,1:T(1,128)} %copy-done.113) | copy-start | bytes 13828
  801.6 608.6 %collective-permute-start.7 = (f32[1,2,6,3,24,128]{5,4,3,2,1,0:T(8,128)}, f32[1,2,6,3,24,128]{5,4,3,2,1,0:T(8,128)}, u32[]{:S(2)}, u32[]{:S(2)}) collective-permute-start(f32[1,2,6,3,24,128]{5,4,3,2,1,0:T(8,128)} %maximum_bitcast_fusion.4), channel_id=1, source_target_pairs={{1,0},{2,1},{3,2},{5,4},{6,5},{7,6},{9,8},{10,9},{11,10},{13,12},{... | collective-permute-start | bytes 1327112 | tf_op jit(solution)/shard_map/ppermute | solution.py:23
  803.2 95.8 %copy-start.63 = (f32[3,24,1,128]{1,2,3,0:T(1,128)S(1)}, f32[3,24,1,128]{1,2,3,0:T(1,128)}, u32[]{:S(2)}) copy-start(f32[3,24,1,128]{1,2,3,0:T(1,128)} %copy-done.62) | copy-start | bytes 110596
  803.6 106.1 %collective-permute-start.4 = (f32[1,2,6,3,384]{4,1,3,2,0:T(2,128)S(1)}, f32[1,2,6,3,384]{4,1,3,2,0:T(2,128)}, u32[]{:S(2)}, u32[]{:S(2)}) collective-permute-start(f32[1,2,6,3,384]{4,1,3,2,0:T(2,128)S(1)} %maximum_bitcast_fusion.8), channel_id=1, source_target_pairs={{0,4},{4,8},{8,12},{12,16},{16,20},{20,24},{24,28},{28,32},{32,36}... | collective-permute-start | bytes 165896 | tf_op jit(solution)/shard_map/ppermute | solution.py:21
  805.8 94.9 %copy-start.8 = (f32[3,24,16,128]{1,3,0,2:T(8,128)S(1)}, f32[3,24,16,128]{1,3,0,2:T(8,128)}, u32[]{:S(2)}) copy-start(f32[3,24,16,128]{1,3,0,2:T(8,128)} %copy-done.7) | copy-start | bytes 1769476
  893.9 19.6 %collective-permute-start.5 = (f32[1,2,6,3,384]{4,1,3,2,0:T(2,128)}, f32[1,2,6,3,384]{4,1,3,2,0:T(2,128)S(1)}, u32[]{:S(2)}, u32[]{:S(2)}) collective-permute-start(f32[1,2,6,3,384]{4,1,3,2,0:T(2,128)} %maximum_bitcast_fusion.9), channel_id=1, source_target_pairs={{4,0},{8,4},{12,8},{16,12},{20,16},{24,20},{28,24},{32,28},{36,32}... | collective-permute-start | bytes 165896 | tf_op jit(solution)/shard_map/ppermute | solution.py:23
  (107 other events, 730.8 us)
Sparse Core Ops, SparseCore 0:
  769.2 638.5 reduce-scatter.1
where the time goes:
time: 1440 us; the launch traced here: 1420 us
  local copies, waits for them, and re-layouts  540 us (38%)
  waiting for transfers between devices  493 us (34%)
  other arithmetic  348 us (24%)
  starting transfers between devices  22.3 us (2%)
  between operations  15.6 us (1%)
    reduce_scatter x1, waiting for transfers between devices, local(): lax.psum_scatter(partial_sums, ('blk', 'span'), scatter_dimension=1, tile...  493 us
    scatter x4, local copies, waits for them, and re-layouts, place(): return jnp.zeros_like(spread).at[:, :, match].set(spread)  154 us
    unnamed x309, local copies, waits for them, and re-layouts  92 us
    sub x10, other arithmetic, interior(): total + jnp.pad(diff, ((0, 0), (0, 0), (0, 0), (0, 1)))  76.6 us
    add x9, other arithmetic, subdomain(): following = 2.0 * current - older + time_step * time_step * total  42.8 us
    sub x34, local copies, waits for them, and re-layouts, subdomain(): current[:, :, :, -1] - older[:, :, :, -1]  36.5 us
    scatter-add x19, other arithmetic, subdomain(): total = total.at[:, :, 0, :].add(phi_s).at[:, :, -1, :].add(phi_n)  35.8 us
    scatter-add x21, local copies, waits for them, and re-layouts, subdomain(): total = total.at[:, :, :, 0].add(phi_w).at[:, :, :, -1].add(phi_e)  34.6 us
  transfers between devices with their start and end apart: 9, of which 1 were waited for; matrix products, arithmetic and copies ran while one was open for 28% of the time, Pallas kernels for 0%

commit v1 on v0

v1 whole, which is shorter than its diff:
```python
import jax
import jax.numpy as jnp
from jax import lax
from jax.experimental import pallas as pl
from jax.experimental.pallas import tpu as pltpu
from jax.sharding import PartitionSpec as P

STEPS = 6
COMPS = 3
THICK = 24
HEIGHT = 16
ARC = 128
FLAT = THICK * HEIGHT
LAYERS = 3
FACE_ROWS = STEPS * COMPS * THICK
PAD_ROWS = 8 * COMPS * THICK
LOAD_ROW = STEPS * COMPS
PATCH_DEV = 32
DEVICES = 128


def roll(values, shift, axis):
    shift %= values.shape[axis]
    return values if shift == 0 else pltpu.roll(values, shift, axis)


def iota(shape, axis):
    return lax.broadcasted_iota(jnp.int32, shape, axis)


def thickness_rows(first, layer, stride=1):
    return pl.ds(first + layer * stride, 8, stride=LAYERS * stride)


def prepare(disp, velocity, modulus, w):
    lane = iota((8, ARC), 1)
    sub = iota((8, ARC), 0)
    zero = jnp.zeros((8, ARC), jnp.float32)
    moduli = [
        roll(modulus[thickness_rows(0, l, HEIGHT), :], 0, 1) for l in range(LAYERS)
    ]
    west = [zero] * LAYERS
    east = [zero] * LAYERS
    for h in range(HEIGHT):
        on_west = lane == h
        on_east = lane == (h - 1) % ARC
        if h + 1 < HEIGHT:
            above = [
                roll(modulus[thickness_rows(h + 1, l, HEIGHT), :], h + 1, 1) for l in range(LAYERS)
            ]
        for l in range(LAYERS):
            m = moduli[l]
            w["along_a"][h, l] = jnp.where(on_east, 0.0, 0.02 * (m + roll(m, -1, 1)))
            if l + 1 < LAYERS:
                w["along_k"][h, l] = 0.02 * (m + moduli[l + 1])
            else:
                w["along_k"][h, l] = jnp.where(sub == 7, 0.0, 0.02 * (m + roll(moduli[0], -1, 0)))
            if h + 1 < HEIGHT:
                w["along_h"][h, l] = 0.02 * (m + roll(above[l], -1, 1))
            imp = jnp.sqrt(m)
            damp = jnp.where(on_west | on_east, imp, 0.0)
            if h == 0:
                damp = damp + imp
                w["faces"][2, l] = 5.0 * imp
            if h == HEIGHT - 1:
                damp = damp + imp
                w["faces"][3, l] = 5.0 * imp
            w["keep"][h, l] = 1.0 - 0.2 * damp
            west[l] = jnp.where(on_west, 5.0 * imp, west[l])
            east[l] = jnp.where(on_east, 5.0 * imp, east[l])
        for c in range(COMPS):
            for l in range(LAYERS):
                rows = thickness_rows(c * THICK * HEIGHT + h, l, HEIGHT)
                w["cur"][h, c * LAYERS + l] = roll(disp[rows, :], h, 1)
                w["vel"][h, c * LAYERS + l] = roll(0.2 * velocity[rows, :], h, 1)
        if h + 1 < HEIGHT:
            moduli = above
    for l in range(LAYERS):
        w["faces"][0, l] = west[l]
        w["faces"][1, l] = east[l]


def record(step, data, sends, w):
    south, south_at, north, north_at = data
    send_south, send_north = sends
    lane = iota((8, ARC), 1)
    zero = jnp.zeros((8, ARC), jnp.float32)
    for c in range(COMPS):
        for l in range(LAYERS):
            b = c * LAYERS + l
            west, east = zero, zero
            for h in range(HEIGHT):
                v = w["vel"][h, b]
                west = jnp.where(lane == h, v, west)
                east = jnp.where(lane == (h - 1) % ARC, v, east)
            rows = thickness_rows(step * (COMPS * THICK) + c * THICK, l)
            g = w["g_west"][rows, :]
            w["inject"][0, b] = 0.04 * g
            w["send_west"][rows, :] = 2.0 * (w["faces"][0, l] * west) - g
            g = w["g_east"][rows, :]
            w["inject"][1, b] = 0.04 * g
            rate = w["faces"][1, l] * east
            w["send_east"][rows, :] = 2.0 * rate - g
            w["load"][b] = w["load"][b] + (g - rate)
            at = thickness_rows(south_at + step * (COMPS * THICK) + c * THICK, l)
            g = south[at, :]
            w["inject"][2, b] = 0.04 * g
            send_south[rows, :] = 2.0 * (w["faces"][2, l] * w["vel"][0, b]) - g
            at = thickness_rows(north_at + step * (COMPS * THICK) + c * THICK, l)
            g = north[at, :]
            w["inject"][3, b] = roll(0.04 * g, HEIGHT - 1, 1)
            rate = w["faces"][3, l] * w["vel"][HEIGHT - 1, b]
            send_north[rows, :] = roll(2.0 * rate, 1 - HEIGHT, 1) - g


def update(w):
    lane = iota((8, ARC), 1)
    blocks = [(c, l) for c in range(COMPS) for l in range(LAYERS)]
    cur = {b: w["cur"][0, b[0] * LAYERS + b[1]] for b in blocks}
    left = {b: roll(cur[b], -1, 1) for b in blocks}
    rising = {}
    for h in range(HEIGHT):
        on_west = lane == h
        on_edge = on_west | (lane == (h - 1) % ARC)
        last = h + 1 == HEIGHT
        cur_next, left_next = {}, {}
        for c in range(COMPS):
            flux_k = []
            for l in range(LAYERS):
                here = cur[c, l]
                over = cur[c, l + 1] if l + 1 < LAYERS else roll(cur[c, 0], -1, 0)
                flux_k.append(w["along_k"][h, l] * (over - here))
            for l in range(LAYERS):
                b = (c, l)
                at = c * LAYERS + l
                here = cur[b]
                flux_a = w["along_a"][h, l] * (left[b] - here)
                total = flux_k[l] - (flux_k[l - 1] if l else roll(flux_k[LAYERS - 1], 1, 0))
                back = flux_a
                if h:
                    back = back + rising[b]
                total = total + flux_a - roll(back, 1, 1)
                if not last:
                    cur_next[b] = w["cur"][h + 1, at]
                    left_next[b] = roll(cur_next[b], -1, 1)
                    rising[b] = w["along_h"][h, l] * (left_next[b] - here)
                    total = total + rising[b]
                g = jnp.where(on_west, w["inject"][0, at], w["inject"][1, at])
                total = total + jnp.where(on_edge, g, 0.0)
                if h == 0:
                    total = total + w["inject"][2, at]
                if last:
                    total = total + w["inject"][3, at]
                v = w["keep"][h, l] * w["vel"][h, at] + total
                w["vel"][h, at] = v
                w["cur"][h, at] = here + v
        cur, left = cur_next, left_next


def gather_rows(history, offset):
    lane = iota((24, ARC), 1)
    parts = []
    for v in range(3):
        part = None
        for t in range(8):
            rows = roll(history[pl.ds(8 * v + t, 24, stride=THICK), :], HEIGHT * t - offset, 1)
            part = rows if part is None else jnp.where(lane >= HEIGHT * t, rows, part)
        parts.append(part)
    return jnp.concatenate(parts, axis=1)


def scatter_rows(flat, history, offset):
    for v in range(3):
        part = flat[:, v * ARC : (v + 1) * ARC]
        for t in range(8):
            history[pl.ds(8 * v + t, 24, stride=THICK), :] = roll(part, offset - HEIGHT * t, 1)


def split(values):
    high = values.astype(jnp.bfloat16)
    rest = values - high.astype(jnp.float32)
    mid = rest.astype(jnp.bfloat16)
    low = (rest - mid.astype(jnp.float32)).astype(jnp.bfloat16)
    return high, mid, low


def pick(values, one_hot, transposed):
    dims = (((1,), (1 if transposed else 0,)), ((), ()))
    total = None
    for part in split(values):
        term = lax.dot_general(part, one_hot, dims, preferred_element_type=jnp.float32)
        total = term if total is None else total + term
    return total


def pairing(match):
    return jnp.where(iota((FLAT, FLAT), 0) == match[...], 1.0, 0.0).astype(jnp.bfloat16)


def sweep(data, sends, w):
    w["load"][...] = jnp.zeros_like(w["load"])

    def one(step, carry):
        record(step, data, sends, w)
        update(w)
        return carry

    lax.fori_loop(0, STEPS - 1, one, 0)
    record(STEPS - 1, data, sends, w)


STATE = ("cur", "vel", "along_a", "along_h", "along_k", "keep", "faces", "inject", "load",
         "g_west", "g_east", "send_west", "send_east")


def state_shapes():
    block = (8, ARC)
    shapes = (
        (HEIGHT, COMPS * LAYERS) + block,
        (HEIGHT, COMPS * LAYERS) + block,
        (HEIGHT, LAYERS) + block,
        (HEIGHT, LAYERS) + block,
        (HEIGHT, LAYERS) + block,
        (HEIGHT, LAYERS) + block,
        (4, LAYERS) + block,
        (4, COMPS * LAYERS) + block,
        (COMPS * LAYERS,) + block,
        (PAD_ROWS, ARC),
        (PAD_ROWS, ARC),
        (PAD_ROWS, ARC),
        (PAD_ROWS, ARC),
    )
    return [pltpu.VMEM(shape, jnp.float32) for shape in shapes]


def clear_tail(w):
    tail = jnp.zeros((PAD_ROWS - FACE_ROWS, ARC), jnp.float32)
    for name in ("send_west", "send_east"):
        w[name][FACE_ROWS:, :] = tail


def first_kernel(disp, velocity, modulus, circ, rising, match, to_left, to_right, to_south, to_north, *scratch):
    w = dict(zip(STATE, scratch))
    prepare(disp, velocity, modulus, w)
    clear_tail(w)
    w["g_west"][0:FACE_ROWS, 0:HEIGHT] = circ[0:FACE_ROWS, :]
    w["g_east"][0:FACE_ROWS, 0:HEIGHT] = circ[FACE_ROWS : 2 * FACE_ROWS, :]
    w["g_east"][0:FACE_ROWS, :] = roll(w["g_east"][0:FACE_ROWS, :], -1, 1)
    sweep((rising, 0, rising, FACE_ROWS), (to_south, to_north), w)
    to_left[...] = pick(gather_rows(w["send_west"], 0), pairing(match), True)
    to_right[...] = gather_rows(w["send_east"], -1)


def second_kernel(
    disp, velocity, modulus, from_left, from_right, south, north, match, owner,
    disp_end, to_left, to_right, to_south, to_north, shares, *scratch
):
    w = dict(zip(STATE, scratch))
    prepare(disp, velocity, modulus, w)
    clear_tail(w)
    one_hot = pairing(match)
    scatter_rows(pick(from_left[...], one_hot, False), w["g_west"], 0)
    scatter_rows(from_right[...], w["g_east"], -1)
    sweep((south, 0, north, 0), (to_south, to_north), w)
    for c in range(COMPS):
        for l in range(LAYERS):
            w["send_east"][thickness_rows(FACE_ROWS + c * THICK, l), :] = w["load"][c * LAYERS + l]
    to_left[...] = pick(gather_rows(w["send_west"], 0), one_hot, True)
    east = gather_rows(w["send_east"], -1)
    to_right[...] = east
    owners = owner[...]
    device = owners // PATCH_DEV
    spot = owners - device * PATCH_DEV
    holder = jnp.where(iota((DEVICES, FLAT), 0) == device, 1.0, 0.0).astype(jnp.bfloat16)
    at = iota((PATCH_DEV, FLAT), 0) == spot
    terms = [
        jnp.where(at, east[LOAD_ROW + c : LOAD_ROW + c + 1, :], 0.0) for c in range(COMPS)
    ]
    terms.append(jnp.zeros((PATCH_DEV, FLAT), jnp.float32))
    total = None
    for part in split(jnp.concatenate(terms, axis=0)):
        term = lax.dot_general(holder, part, (((1,), (1,)), ((), ())), preferred_element_type=jnp.float32)
        total = term if total is None else total + term
    shares[...] = total
    update(w)
    for h in range(HEIGHT):
        for c in range(COMPS):
            for l in range(LAYERS):
                rows = thickness_rows(c * THICK * HEIGHT + h, l, HEIGHT)
                disp_end[rows, :] = roll(w["cur"][h, c * LAYERS + l], -h, 1)


def third_kernel(from_left, from_right, south, north, match, shares, circ_next, height_next, patch_load, rows, sems):
    copies = [
        pltpu.make_async_copy(south, height_next.at[pl.ds(0, FACE_ROWS)], sems.at[0]),
        pltpu.make_async_copy(north, height_next.at[pl.ds(FACE_ROWS, FACE_ROWS)], sems.at[1]),
    ]
    for copy in copies:
        copy.start()
    scatter_rows(pick(from_left[...], pairing(match), False), rows, 0)
    circ_next[0:FACE_ROWS, :] = rows[0:FACE_ROWS, 0:HEIGHT]
    scatter_rows(from_right[...], rows, 0)
    circ_next[FACE_ROWS : 2 * FACE_ROWS, :] = rows[0:FACE_ROWS, 0:HEIGHT]
    total = jnp.sum(shares[...], axis=0, keepdims=True)
    for c in range(COMPS):
        patch_load[c : c + 1, :] = total[:, c * PATCH_DEV : (c + 1) * PATCH_DEV]
    for copy in copies:
        copy.wait()


def f32(*shape):
    return jax.ShapeDtypeStruct(shape, jnp.float32)


PARAMS = pltpu.CompilerParams(vmem_limit_bytes=24 * 1024 * 1024)
VMEM = pl.BlockSpec(memory_space=pltpu.VMEM)
ANY = pl.BlockSpec(memory_space=pl.ANY)


def routed(to_left, to_right, to_south, to_north):
    blks, spans = lax.axis_size("blk"), lax.axis_size("span")
    south = lax.ppermute(to_north, "span", [(i, i + 1) for i in range(spans - 1)])
    north = lax.ppermute(to_south, "span", [(i + 1, i) for i in range(spans - 1)])
    west = lax.ppermute(to_right, "blk", [(i, (i + 1) % blks) for i in range(blks)])
    east = lax.ppermute(to_left, "blk", [((i + 1) % blks, i) for i in range(blks)])
    return west, east, south, north


def local(disp, velocity, modulus, guess_circ, guess_height, pair_match, patch_owner):
    disp = disp.reshape(COMPS * FLAT, ARC)
    velocity = velocity.reshape(COMPS * FLAT, ARC)
    modulus = modulus.reshape(FLAT, ARC)
    circ = guess_circ.reshape(2 * FACE_ROWS, HEIGHT)
    rising = guess_height.reshape(2 * FACE_ROWS, ARC)
    match = pair_match.reshape(1, FLAT)
    owner = patch_owner.reshape(1, FLAT)
    face = f32(FACE_ROWS, ARC)
    flat = f32(24, FLAT)
    sends = pl.pallas_call(
        first_kernel,
        out_shape=(flat, flat, face, face),
        in_specs=[VMEM] * 6,
        out_specs=(VMEM,) * 4,
        scratch_shapes=state_shapes(),
        compiler_params=PARAMS,
    )(disp, velocity, modulus, circ, rising, match)
    west, east, south, north = routed(*sends)
    disp_end, *sends, shares = pl.pallas_call(
        second_kernel,
        out_shape=(f32(COMPS * FLAT, ARC), flat, flat, face, face, f32(DEVICES, ARC)),
        in_specs=[VMEM] * 9,
        out_specs=(VMEM,) * 6,
        scratch_shapes=state_shapes(),
        compiler_params=PARAMS,
    )(disp, velocity, modulus, west, east, south, north, match, owner)
    west, east, south, north = routed(*sends)
    shares = lax.all_to_all(shares, ("blk", "span"), split_axis=0, concat_axis=0, tiled=True)
    circ_next, height_next, patch_load = pl.pallas_call(
        third_kernel,
        out_shape=(f32(2 * FACE_ROWS, HEIGHT), f32(2 * FACE_ROWS, ARC), f32(COMPS, PATCH_DEV)),
        in_specs=[VMEM, VMEM, ANY, ANY, VMEM, VMEM],
        out_specs=(VMEM, ANY, VMEM),
        scratch_shapes=[pltpu.VMEM((PAD_ROWS, ARC), jnp.float32), pltpu.SemaphoreType.DMA((2,))],
        compiler_params=PARAMS,
    )(west, east, south, north, match, shares)
    return (
        disp_end.reshape(COMPS, THICK, HEIGHT, ARC),
        circ_next.reshape(1, 2, STEPS, COMPS, THICK, HEIGHT),
        height_next.reshape(1, 2, STEPS, COMPS, THICK, ARC),
        patch_load,
    )


def solution(mesh):
    in_specs = (
        P(None, None, "span", "blk"),
        P(None, None, "span", "blk"),
        P(None, "span", "blk"),
        P("blk", None, None, None, None, "span"),
        P("span", None, None, None, None, "blk"),
        P("blk", "span", None),
        P("blk", "span", None),
    )
    out_specs = (
        P(None, None, "span", "blk"),
        P("blk", None, None, None, None, "span"),
        P("span", None, None, None, None, "blk"),
        P(None, ("blk", "span")),
    )
    return jax.shard_map(local, mesh=mesh, in_specs=in_specs, out_specs=out_specs, check_vma=False)
```

time: 1440 us -> 58.8 us (0.04)
  the two profiles are of different devices: /device:TPU:0 before, /device:TPU:1 now
where the time goes in v1:
time: 58.8 us; the launch traced here: 58.4 us
  starting transfers between devices  27 us (46%)
  Pallas kernels  12.9 us (22%)
  waiting for transfers between devices  12 us (20%)
  local copies, waits for them, and re-layouts  5.79 us (10%)
  between operations  0.74 us (1%)
    all_to_all x1, starting transfers between devices, local(): lax.all_to_all(shares, ('blk', 'span'), split_axis=0, concat_axis=0, tile...  12.2 us
    ppermute x2, starting transfers between devices, routed(): lax.ppermute(to_north, 'span', [(i, i + 1) for i in range(spans - 1)])  7.9 us
    pallas_call x1, Pallas kernels, local(): pl.pallas_call(second_kernel, out_shape=(f32(COMPS * FLAT, ARC), flat, fl...  6.37 us
    unnamed x14, local copies, waits for them, and re-layouts  5.79 us
    ppermute x2, waiting for transfers between devices, routed(): lax.ppermute(to_left, 'blk', [((i + 1) % blks, i) for i in range(blks)])  5.37 us
    pallas_call x1, Pallas kernels, local(): pl.pallas_call(first_kernel, out_shape=(flat, flat, face, face), in_specs...  4.83 us
    ppermute x2, starting transfers between devices, routed(): lax.ppermute(to_right, 'blk', [(i, (i + 1) % blks) for i in range(blks)])  4.37 us
    all_to_all x1, waiting for transfers between devices, local(): lax.all_to_all(shares, ('blk', 'span'), split_axis=0, concat_axis=0, tile...  4.18 us
  transfers between devices with their start and end apart: 9, of which 6 were waited for; matrix products, arithmetic and copies ran while one was open for 0% of the time, Pallas kernels for 0%

profile of v1, /device:TPU:1, one launch (start us, length us, event | category | flops | bytes accessed | tf_op | source)
XLA Modules:
  0.0 58.4 jit_solution(6959885821574195010)
XLA Ops:
  0.6 1.2 %copy.13 = f32[1,2,6,3,24,16]{5,4,3,2,1,0:T(8,128)S(1)} copy(f32[1,2,6,3,24,16]{4,5,3,2,1,0:T(8,128)} %param.10) | data formatting | bytes 110592 | tf_op args[3]
  1.9 0.0 copy-start.4
  1.9 0.7 %copy-done.4 = s32[1,1,384]{2,1,0:T(1,128)S(1)} copy-done((s32[1,1,384]{2,1,0:T(1,128)S(1)}, s32[1,1,384]{2,1,0:T(1,128)}, u32[]{:S(2)}) %copy-start.4) | copy-done | bytes 1560
  2.6 1.1 %copy-done.1 = f32[3,24,16,128]{3,2,1,0:T(8,128)S(1)} copy-done((f32[3,24,16,128]{3,2,1,0:T(8,128)S(1)}, f32[3,24,16,128]{3,2,1,0:T(8,128)}, u32[]{:S(2)}) %copy-start.1) | copy-done | bytes 589848
  3.6 0.9 %copy-done.2 = f32[24,16,128]{2,1,0:T(8,128)S(1)} copy-done((f32[24,16,128]{2,1,0:T(8,128)S(1)}, f32[24,16,128]{2,1,0:T(8,128)}, u32[]{:S(2)}) %copy-start.2) | copy-done | bytes 196632
  4.5 1.0 %copy-done.3 = f32[1,2,6,3,24,128]{5,4,3,2,1,0:T(8,128)S(1)} copy-done((f32[1,2,6,3,24,128]{5,4,3,2,1,0:T(8,128)S(1)}, f32[1,2,6,3,24,128]{5,4,3,2,1,0:T(8,128)}, u32[]{:S(2)}) %copy-start.3) | copy-done | bytes 442392
  5.6 4.8 %shard_map.102 = (f32[24,384]{1,0:T(8,128)S(1)}, f32[24,384]{1,0:T(8,128)S(1)}, f32[432,128]{1,0:T(8,128)S(1)}, f32[432,128]{1,0:T(8,128)S(1)}) custom-call(f32[1152,128]{1,0:T(8,128)S(1)} %bitcast.14, f32[1152,128]{1,0:T(8,128)S(1)} %bitcast.16, f32[384,128]{1,0:T(8,128)S(1)} %bitcast.19, f32[864,16]{1,0:T(8,128)S(1)} %bitcast.18, f32[864,128]{1,0:T(8,128)S(1)} %bitcast.21, ...), custom_call_target="tpu_custom_call" | custom-call | tf_op jit(solution)/shard_map/pallas_call | solution.py:339
  10.4 4.0 %collective-permute-start.2 = (f32[432,128]{1,0:T(8,128)S(1)}, f32[432,128]{1,0:T(8,128)S(1)}, u32[]{:S(2)}, u32[]{:S(2)}) collective-permute-start(f32[432,128]{1,0:T(8,128)S(1)} %get-tuple-element.19), channel_id=1, source_target_pairs={{0,1},{1,2},{2,3},{4,5},{5,6},{6,7},{8,9},{9,10},{10,11},{12,13},{... | collective-permute-start | bytes 663560 | tf_op jit(solution)/shard_map/ppermute | solution.py:322
  14.4 1.3 %collective-permute-start.3 = (f32[432,128]{1,0:T(8,128)S(1)}, f32[432,128]{1,0:T(8,128)S(1)}, u32[]{:S(2)}, u32[]{:S(2)}) collective-permute-start(f32[432,128]{1,0:T(8,128)S(1)} %get-tuple-element.20), channel_id=1, source_target_pairs={{1,0},{2,1},{3,2},{5,4},{6,5},{7,6},{9,8},{10,9},{11,10},{13,12},{... | collective-permute-start | bytes 663560 | tf_op jit(solution)/shard_map/ppermute | solution.py:323
  15.7 0.0 copy-start.5
  15.7 2.5 %collective-permute-start = (f32[24,384]{1,0:T(8,128)S(1)}, f32[24,384]{1,0:T(8,128)S(1)}, u32[]{:S(2)}, u32[]{:S(2)}) collective-permute-start(f32[24,384]{1,0:T(8,128)S(1)} %get-tuple-element.17), channel_id=1, source_target_pairs={{0,4},{4,8},{8,12},{12,16},{16,20},{20,24},{24,28},{28,32},{32,36}... | collective-permute-start | bytes 110600 | tf_op jit(solution)/shard_map/ppermute | solution.py:324
  18.2 1.1 %collective-permute-done.from_left = f32[24,384]{1,0:T(8,128)S(1)} collective-permute-done((f32[24,384]{1,0:T(8,128)S(1)}, f32[24,384]{1,0:T(8,128)S(1)}, u32[]{:S(2)}, u32[]{:S(2)}) %collective-permute-start) | collective-permute-done | bytes 36896 | tf_op jit(solution)/shard_map/ppermute | solution.py:324
  19.3 2.6 %collective-permute-done.1.from_right = f32[24,384]{1,0:T(8,128)S(1)} collective-permute-done((f32[24,384]{1,0:T(8,128)S(1)}, f32[24,384]{1,0:T(8,128)S(1)}, u32[]{:S(2)}, u32[]{:S(2)}) %collective-permute-start.1) | collective-permute-done | bytes 36896 | tf_op jit(solution)/shard_map/ppermute | solution.py:325
  21.9 0.3 collective-permute-done.3.north
  22.2 6.4 %shard_map.103 = (f32[1152,128]{1,0:T(8,128)}, f32[24,384]{1,0:T(8,128)S(1)}, f32[24,384]{1,0:T(8,128)S(1)}, f32[432,128]{1,0:T(8,128)S(1)}, f32[432,128]{1,0:T(8,128)S(1)}, /*index=5*/f32[128,128]{1,0:T(8,128)}) custom-call(f32[1152,128]{1,0:T(8,128)S(1)} %bitcast.15, f32[1152,128]{1,0:T(8,128)S(1)} %bitcast.17, f32[384,128]{1,0:T(8,128)S(1)} %bitcast.20, ...), custom_call_target="tpu_custom_call" | custom-call | tf_op jit(solution)/shard_map/pallas_call | solution.py:348
  28.6 3.9 %collective-permute-start.6 = (f32[432,128]{1,0:T(8,128)S(1)}, f32[432,128]{1,0:T(8,128)S(1)}, u32[]{:S(2)}, u32[]{:S(2)}) collective-permute-start(f32[432,128]{1,0:T(8,128)S(1)} %get-tuple-element.24), channel_id=1, source_target_pairs={{0,1},{1,2},{2,3},{4,5},{5,6},{6,7},{8,9},{9,10},{10,11},{12,13},{... | collective-permute-start | bytes 663560 | tf_op jit(solution)/shard_map/ppermute | solution.py:322
  32.6 1.3 %collective-permute-start.7 = (f32[432,128]{1,0:T(8,128)S(1)}, f32[432,128]{1,0:T(8,128)S(1)}, u32[]{:S(2)}, u32[]{:S(2)}) collective-permute-start(f32[432,128]{1,0:T(8,128)S(1)} %get-tuple-element.25), channel_id=1, source_target_pairs={{1,0},{2,1},{3,2},{5,4},{6,5},{7,6},{9,8},{10,9},{11,10},{13,12},{... | collective-permute-start | bytes 663560 | tf_op jit(solution)/shard_map/ppermute | solution.py:323
  33.9 12.2 %all-to-all-start = ((f32[128,1,128]{2,1,0:T(1,128)}), f32[128,1,128]{2,1,0:T(1,128)S(1)}, u32[]{:S(2)}, u32[]{:S(2)}) async-start(f32[128,1,128]{2,1,0:T(1,128)} %bitcast.9), calls=%async_computation | async-start | bytes 131072 | tf_op jit(solution)/shard_map/all_to_all | solution.py:357
  46.0 1.8 %collective-permute-start.4 = (f32[24,384]{1,0:T(8,128)S(1)}, f32[24,384]{1,0:T(8,128)S(1)}, u32[]{:S(2)}, u32[]{:S(2)}) collective-permute-start(f32[24,384]{1,0:T(8,128)S(1)} %get-tuple-element.22), channel_id=1, source_target_pairs={{0,4},{4,8},{8,12},{12,16},{16,20},{20,24},{24,28},{28,32},{32,36}... | collective-permute-start | bytes 110600 | tf_op jit(solution)/shard_map/ppermute | solution.py:324
  47.8 1.1 %collective-permute-done.4.from_left = f32[24,384]{1,0:T(8,128)S(1)} collective-permute-done((f32[24,384]{1,0:T(8,128)S(1)}, f32[24,384]{1,0:T(8,128)S(1)}, u32[]{:S(2)}, u32[]{:S(2)}) %collective-permute-start.4) | collective-permute-done | bytes 36896 | tf_op jit(solution)/shard_map/ppermute | solution.py:324
  48.9 2.8 %collective-permute-done.5.from_right = f32[24,384]{1,0:T(8,128)S(1)} collective-permute-done((f32[24,384]{1,0:T(8,128)S(1)}, f32[24,384]{1,0:T(8,128)S(1)}, u32[]{:S(2)}, u32[]{:S(2)}) %collective-permute-start.5) | collective-permute-done | bytes 36896 | tf_op jit(solution)/shard_map/ppermute | solution.py:325
  51.7 4.2 %all-to-all-done = f32[128,1,128]{2,1,0:T(1,128)S(1)} async-done(((f32[128,1,128]{2,1,0:T(1,128)}), f32[128,1,128]{2,1,0:T(1,128)S(1)}, u32[]{:S(2)}, u32[]{:S(2)}) %all-to-all-start) | async-done | bytes 65568 | tf_op jit(solution)/shard_map/all_to_all | solution.py:357
  55.8 1.7 %shard_map.104 = (f32[864,16]{1,0:T(8,128)S(1)}, f32[864,128]{1,0:T(8,128)}, f32[3,32]{1,0:T(4,128)}) custom-call(f32[24,384]{1,0:T(8,128)S(1)} %collective-permute-done.4.from_left, f32[24,384]{1,0:T(8,128)S(1)} %collective-permute-done.5.from_right, f32[432,128]{1,0:T(8,128)S(1)} %collective-permute-done.6.south, ...), custom_call_target="tpu_custom_call" | custom-call | tf_op jit(solution)/shard_map/pallas_call | solution.py:358
  57.5 0.9 %copy.15 = f32[1,2,6,3,24,16]{4,5,3,2,1,0:T(8,128)} copy(f32[1,2,6,3,24,16]{5,4,3,2,1,0:T(8,128)S(1)} %bitcast.22) | data formatting | bytes 110592
  (11 shorter events, 0.0 us)
Async XLA Ops:
  0.6 1.2 %copy-start = (f32[3,24,16,128]{3,2,1,0:T(8,128)S(1)}, f32[3,24,16,128]{3,2,1,0:T(8,128)}, u32[]{:S(2)}) copy-start(f32[3,24,16,128]{3,2,1,0:T(8,128)} %param.7) | copy-start | bytes 1769476
  1.9 0.7 %copy-start.4 = (s32[1,1,384]{2,1,0:T(1,128)S(1)}, s32[1,1,384]{2,1,0:T(1,128)}, u32[]{:S(2)}) copy-start(s32[1,1,384]{2,1,0:T(1,128)} %param.12) | copy-start | bytes 4612
  2.6 1.1 %copy-start.1 = (f32[3,24,16,128]{3,2,1,0:T(8,128)S(1)}, f32[3,24,16,128]{3,2,1,0:T(8,128)}, u32[]{:S(2)}) copy-start(f32[3,24,16,128]{3,2,1,0:T(8,128)} %param.8) | copy-start | bytes 1769476
  3.6 0.9 %copy-start.2 = (f32[24,16,128]{2,1,0:T(8,128)S(1)}, f32[24,16,128]{2,1,0:T(8,128)}, u32[]{:S(2)}) copy-start(f32[24,16,128]{2,1,0:T(8,128)} %param.9) | copy-start | bytes 589828
  4.5 1.0 %copy-start.3 = (f32[1,2,6,3,24,128]{5,4,3,2,1,0:T(8,128)S(1)}, f32[1,2,6,3,24,128]{5,4,3,2,1,0:T(8,128)}, u32[]{:S(2)}) copy-start(f32[1,2,6,3,24,128]{5,4,3,2,1,0:T(8,128)} %param.11) | copy-start | bytes 1327108
  10.4 11.5 %collective-permute-start.2 = (f32[432,128]{1,0:T(8,128)S(1)}, f32[432,128]{1,0:T(8,128)S(1)}, u32[]{:S(2)}, u32[]{:S(2)}) collective-permute-start(f32[432,128]{1,0:T(8,128)S(1)} %get-tuple-element.19), channel_id=1, source_target_pairs={{0,1},{1,2},{2,3},{4,5},{5,6},{6,7},{8,9},{9,10},{10,11},{12,13},{... | collective-permute-start | bytes 663560 | tf_op jit(solution)/shard_map/ppermute | solution.py:322
  14.4 7.9 %collective-permute-start.3 = (f32[432,128]{1,0:T(8,128)S(1)}, f32[432,128]{1,0:T(8,128)S(1)}, u32[]{:S(2)}, u32[]{:S(2)}) collective-permute-start(f32[432,128]{1,0:T(8,128)S(1)} %get-tuple-element.20), channel_id=1, source_target_pairs={{1,0},{2,1},{3,2},{5,4},{6,5},{7,6},{9,8},{10,9},{11,10},{13,12},{... | collective-permute-start | bytes 663560 | tf_op jit(solution)/shard_map/ppermute | solution.py:323
  15.7 6.6 %copy-start.5 = (s32[1,1,384]{2,1,0:T(1,128)S(1)}, s32[1,1,384]{2,1,0:T(1,128)}, u32[]{:S(2)}) copy-start(s32[1,1,384]{2,1,0:T(1,128)} %param.13) | copy-start | bytes 4612
  15.7 3.6 %collective-permute-start = (f32[24,384]{1,0:T(8,128)S(1)}, f32[24,384]{1,0:T(8,128)S(1)}, u32[]{:S(2)}, u32[]{:S(2)}) collective-permute-start(f32[24,384]{1,0:T(8,128)S(1)} %get-tuple-element.17), channel_id=1, source_target_pairs={{0,4},{4,8},{8,12},{12,16},{16,20},{20,24},{24,28},{28,32},{32,36}... | collective-permute-start | bytes 110600 | tf_op jit(solution)/shard_map/ppermute | solution.py:324
  18.2 3.7 %collective-permute-start.1 = (f32[24,384]{1,0:T(8,128)S(1)}, f32[24,384]{1,0:T(8,128)S(1)}, u32[]{:S(2)}, u32[]{:S(2)}) collective-permute-start(f32[24,384]{1,0:T(8,128)S(1)} %get-tuple-element.18), channel_id=1, source_target_pairs={{4,0},{8,4},{12,8},{16,12},{20,16},{24,20},{28,24},{32,28},{36,32}... | collective-permute-start | bytes 110600 | tf_op jit(solution)/shard_map/ppermute | solution.py:325
  28.6 27.2 %collective-permute-start.6 = (f32[432,128]{1,0:T(8,128)S(1)}, f32[432,128]{1,0:T(8,128)S(1)}, u32[]{:S(2)}, u32[]{:S(2)}) collective-permute-start(f32[432,128]{1,0:T(8,128)S(1)} %get-tuple-element.24), channel_id=1, source_target_pairs={{0,1},{1,2},{2,3},{4,5},{5,6},{6,7},{8,9},{9,10},{10,11},{12,13},{... | collective-permute-start | bytes 663560 | tf_op jit(solution)/shard_map/ppermute | solution.py:322
  32.6 23.3 %collective-permute-start.7 = (f32[432,128]{1,0:T(8,128)S(1)}, f32[432,128]{1,0:T(8,128)S(1)}, u32[]{:S(2)}, u32[]{:S(2)}) collective-permute-start(f32[432,128]{1,0:T(8,128)S(1)} %get-tuple-element.25), channel_id=1, source_target_pairs={{1,0},{2,1},{3,2},{5,4},{6,5},{7,6},{9,8},{10,9},{11,10},{13,12},{... | collective-permute-start | bytes 663560 | tf_op jit(solution)/shard_map/ppermute | solution.py:323
  33.9 22.0 %all-to-all-start = ((f32[128,1,128]{2,1,0:T(1,128)}), f32[128,1,128]{2,1,0:T(1,128)S(1)}, u32[]{:S(2)}, u32[]{:S(2)}) async-start(f32[128,1,128]{2,1,0:T(1,128)} %bitcast.9), calls=%async_computation | async-start | bytes 131072 | tf_op jit(solution)/shard_map/all_to_all | solution.py:357
  46.0 2.9 %collective-permute-start.4 = (f32[24,384]{1,0:T(8,128)S(1)}, f32[24,384]{1,0:T(8,128)S(1)}, u32[]{:S(2)}, u32[]{:S(2)}) collective-permute-start(f32[24,384]{1,0:T(8,128)S(1)} %get-tuple-element.22), channel_id=1, source_target_pairs={{0,4},{4,8},{8,12},{12,16},{16,20},{20,24},{24,28},{28,32},{32,36}... | collective-permute-start | bytes 110600 | tf_op jit(solution)/shard_map/ppermute | solution.py:324
  47.8 3.8 %collective-permute-start.5 = (f32[24,384]{1,0:T(8,128)S(1)}, f32[24,384]{1,0:T(8,128)S(1)}, u32[]{:S(2)}, u32[]{:S(2)}) collective-permute-start(f32[24,384]{1,0:T(8,128)S(1)} %get-tuple-element.23), channel_id=1, source_target_pairs={{4,0},{8,4},{12,8},{16,12},{20,16},{24,20},{28,24},{32,28},{36,32}... | collective-permute-start | bytes 110600 | tf_op jit(solution)/shard_map/ppermute | solution.py:325

commit v2 on v1

--- a/solution.py
+++ b/solution.py
@@ -32,7 +32,7 @@
     return pl.ds(first + layer * stride, 8, stride=LAYERS * stride)
 
 
-def prepare(disp, velocity, modulus, w):
+def coefficients(modulus, w):
     lane = iota((8, ARC), 1)
     sub = iota((8, ARC), 0)
     zero = jnp.zeros((8, ARC), jnp.float32)
@@ -68,11 +68,6 @@
             w["keep"][h, l] = 1.0 - 0.2 * damp
             west[l] = jnp.where(on_west, 5.0 * imp, west[l])
             east[l] = jnp.where(on_east, 5.0 * imp, east[l])
-        for c in range(COMPS):
-            for l in range(LAYERS):
-                rows = thickness_rows(c * THICK * HEIGHT + h, l, HEIGHT)
-                w["cur"][h, c * LAYERS + l] = roll(disp[rows, :], h, 1)
-                w["vel"][h, c * LAYERS + l] = roll(0.2 * velocity[rows, :], h, 1)
         if h + 1 < HEIGHT:
             moduli = above
     for l in range(LAYERS):
@@ -80,9 +75,32 @@
         w["faces"][1, l] = east[l]
 
 
+def load_state(source, scale, kept, used):
+    for h in range(HEIGHT):
+        for c in range(COMPS):
+            for l in range(LAYERS):
+                rows = thickness_rows(c * THICK * HEIGHT + h, l, HEIGHT)
+                values = source[rows, :]
+                if scale != 1.0:
+                    values = scale * values
+                values = roll(values, h, 1)
+                kept[h, c * LAYERS + l] = values
+                used[h, c * LAYERS + l] = values
+
+
+def sides():
+    east = lax.axis_index("blk") % 2 == 0
+    span = lax.axis_index("span")
+    north = span % 2 == 0
+    inner = (span > 0) & (span + 1 < lax.axis_size("span"))
+    return east, north, inner
+
+
 def record(step, data, sends, w):
-    south, south_at, north, north_at = data
-    send_south, send_north = sends
+    south_of, north_of = data
+    send_first, send_second = sends
+    _, to_north, inner = sides()
+    weight = jnp.where(inner, 1.0, 0.0)
     lane = iota((8, ARC), 1)
     zero = jnp.zeros((8, ARC), jnp.float32)
     for c in range(COMPS):
@@ -102,21 +120,23 @@
             rate = w["faces"][1, l] * east
             w["send_east"][rows, :] = 2.0 * rate - g
             w["load"][b] = w["load"][b] + (g - rate)
-            at = thickness_rows(south_at + step * (COMPS * THICK) + c * THICK, l)
-            g = south[at, :]
+            g = south_of(rows, step * (COMPS * THICK) + c * THICK, l)
             w["inject"][2, b] = 0.04 * g
-            send_south[rows, :] = 2.0 * (w["faces"][2, l] * w["vel"][0, b]) - g
-            at = thickness_rows(north_at + step * (COMPS * THICK) + c * THICK, l)
-            g = north[at, :]
+            south = 2.0 * (w["faces"][2, l] * w["vel"][0, b]) - g
+            g = north_of(rows, step * (COMPS * THICK) + c * THICK, l)
             w["inject"][3, b] = roll(0.04 * g, HEIGHT - 1, 1)
             rate = w["faces"][3, l] * w["vel"][HEIGHT - 1, b]
-            send_north[rows, :] = roll(2.0 * rate, 1 - HEIGHT, 1) - g
-
-
-def update(w):
+            north = roll(2.0 * rate, 1 - HEIGHT, 1) - g
+            send_first[rows, :] = jnp.where(to_north, north, south)
+            send_second[rows, :] = weight * jnp.where(to_north, south, north)
+
+
+def update(w, from_cur=None, from_vel=None, sink=None):
+    from_cur = w["cur"] if from_cur is None else from_cur
+    from_vel = w["vel"] if from_vel is None else from_vel
     lane = iota((8, ARC), 1)
     blocks = [(c, l) for c in range(COMPS) for l in range(LAYERS)]
-    cur = {b: w["cur"][0, b[0] * LAYERS + b[1]] for b in blocks}
+    cur = {b: from_cur[0, b[0] * LAYERS + b[1]] for b in blocks}
     left = {b: roll(cur[b], -1, 1) for b in blocks}
     rising = {}
     for h in range(HEIGHT):
@@ -141,7 +161,7 @@
                     back = back + rising[b]
                 total = total + flux_a - roll(back, 1, 1)
                 if not last:
-                    cur_next[b] = w["cur"][h + 1, at]
+                    cur_next[b] = from_cur[h + 1, at]
                     left_next[b] = roll(cur_next[b], -1, 1)
                     rising[b] = w["along_h"][h, l] * (left_next[b] - here)
                     total = total + rising[b]
@@ -151,9 +171,12 @@
                     total = total + w["inject"][2, at]
                 if last:
                     total = total + w["inject"][3, at]
-                v = w["keep"][h, l] * w["vel"][h, at] + total
-                w["vel"][h, at] = v
-                w["cur"][h, at] = here + v
+                v = w["keep"][h, l] * from_vel[h, at] + total
+                if sink is None:
+                    w["vel"][h, at] = v
+                    w["cur"][h, at] = here + v
+                else:
+                    sink(h, at, here + v)
         cur, left = cur_next, left_next
 
 
@@ -209,27 +232,16 @@
     record(STEPS - 1, data, sends, w)
 
 
-STATE = ("cur", "vel", "along_a", "along_h", "along_k", "keep", "faces", "inject", "load",
-         "g_west", "g_east", "send_west", "send_east")
-
-
-def state_shapes():
-    block = (8, ARC)
-    shapes = (
-        (HEIGHT, COMPS * LAYERS) + block,
-        (HEIGHT, COMPS * LAYERS) + block,
-        (HEIGHT, LAYERS) + block,
-        (HEIGHT, LAYERS) + block,
-        (HEIGHT, LAYERS) + block,
-        (HEIGHT, LAYERS) + block,
-        (4, LAYERS) + block,
-        (4, COMPS * LAYERS) + block,
-        (COMPS * LAYERS,) + block,
-        (PAD_ROWS, ARC),
-        (PAD_ROWS, ARC),
-        (PAD_ROWS, ARC),
-        (PAD_ROWS, ARC),
-    )
+WORK = ("inject", "load", "g_west", "g_east", "send_west", "send_east")
+COEFFICIENTS = ("along_a", "along_h", "along_k", "keep", "faces")
+BLOCK = (8, ARC)
+STATE_SHAPE = (HEIGHT, COMPS * LAYERS) + BLOCK
+COEFFICIENT_SHAPES = ((HEIGHT, LAYERS) + BLOCK,) * 4 + ((4, LAYERS) + BLOCK,)
+INJECT_SHAPE = (4, COMPS * LAYERS) + BLOCK
+
+
+def work_shapes():
+    shapes = (INJECT_SHAPE, (COMPS * LAYERS,) + BLOCK) + ((PAD_ROWS, ARC),) * 4
     return [pltpu.VMEM(shape, jnp.float32) for shape in shapes]
 
 
@@ -239,35 +251,86 @@
         w[name][FACE_ROWS:, :] = tail
 
 
-def first_kernel(disp, velocity, modulus, circ, rising, match, to_left, to_right, to_south, to_north, *scratch):
-    w = dict(zip(STATE, scratch))
-    prepare(disp, velocity, modulus, w)
+def spread_guess(circ, side, history, offset):
+    rows = STEPS * COMPS * HEIGHT
+    unit = jnp.where(iota((THICK, THICK), 0) == iota((THICK, THICK), 1), 1.0, 0.0).astype(jnp.bfloat16)
+    total = None
+    for part in split(circ[side * rows : (side + 1) * rows, :]):
+        term = lax.dot_general(unit, part, (((1,), (1,)), ((), ())), preferred_element_type=jnp.float32)
+        total = term if total is None else total + term
+    total = jnp.concatenate([total, jnp.zeros((THICK, 3 * ARC - rows), jnp.float32)], axis=1)
+    for i in range(STEPS * COMPS):
+        tile = total[:, i // 8 * ARC : (i // 8 + 1) * ARC]
+        history[i * THICK : (i + 1) * THICK, :] = roll(tile, offset - HEIGHT * (i % 8), 1)
+
+
+def first_kernel(disp, velocity, modulus, circ, rising, pair_match, patch_owner, *refs):
+    first_c, second_c, first_h, second_h, match, owner, cur0, vel0 = refs[:8]
+    w = dict(zip(COEFFICIENTS, refs[8:13]))
+    disp_in, velocity_in, modulus_in, circ_in, rising_in, sems, w["cur"], w["vel"] = refs[13:21]
+    w.update(zip(WORK, refs[21:]))
+    copies = [
+        pltpu.make_async_copy(source, target, sems.at[i])
+        for i, (source, target) in enumerate(
+            (
+                (modulus, modulus_in),
+                (velocity, velocity_in),
+                (disp, disp_in),
+                (circ, circ_in),
+                (rising, rising_in),
+                (pair_match, match),
+                (patch_owner, owner),
+            )
+        )
+    ]
+    for copy in copies:
+        copy.start()
     clear_tail(w)
-    w["g_west"][0:FACE_ROWS, 0:HEIGHT] = circ[0:FACE_ROWS, :]
-    w["g_east"][0:FACE_ROWS, 0:HEIGHT] = circ[FACE_ROWS : 2 * FACE_ROWS, :]
-    w["g_east"][0:FACE_ROWS, :] = roll(w["g_east"][0:FACE_ROWS, :], -1, 1)
-    sweep((rising, 0, rising, FACE_ROWS), (to_south, to_north), w)
-    to_left[...] = pick(gather_rows(w["send_west"], 0), pairing(match), True)
-    to_right[...] = gather_rows(w["send_east"], -1)
-
-
-def second_kernel(
-    disp, velocity, modulus, from_left, from_right, south, north, match, owner,
-    disp_end, to_left, to_right, to_south, to_north, shares, *scratch
-):
-    w = dict(zip(STATE, scratch))
-    prepare(disp, velocity, modulus, w)
+    copies[0].wait()
+    coefficients(modulus_in, w)
+    copies[1].wait()
+    load_state(velocity_in, 0.2, vel0, w["vel"])
+    copies[2].wait()
+    load_state(disp_in, 1.0, cur0, w["cur"])
+    copies[3].wait()
+    spread_guess(circ_in, 0, w["g_west"], 0)
+    spread_guess(circ_in, 1, w["g_east"], -1)
+    for copy in copies[4:]:
+        copy.wait()
+    data = (
+        lambda rows, at, l: rising_in[thickness_rows(at, l), :],
+        lambda rows, at, l: rising_in[thickness_rows(FACE_ROWS + at, l), :],
+    )
+    sweep(data, (first_h, second_h), w)
+    west = pick(gather_rows(w["send_west"], 0), pairing(match), True)
+    east = gather_rows(w["send_east"], -1)
+    to_east, _, _ = sides()
+    first_c[...] = jnp.where(to_east, east, west)
+    second_c[...] = jnp.where(to_east, west, east)
+
+
+def second_kernel(got_first_c, got_second_c, got_first_h, got_second_h, match, owner, cur0, vel0, *refs):
+    w = dict(zip(COEFFICIENTS, refs[:5]))
+    first_c, second_c, first_h, second_h, shares, inject, w["cur"], w["vel"] = refs[5:13]
+    w.update(zip(WORK, (inject,) + refs[13:]))
     clear_tail(w)
     one_hot = pairing(match)
-    scatter_rows(pick(from_left[...], one_hot, False), w["g_west"], 0)
-    scatter_rows(from_right[...], w["g_east"], -1)
-    sweep((south, 0, north, 0), (to_south, to_north), w)
+    to_east, to_north, _ = sides()
+    first, second = got_first_c[...], got_second_c[...]
+    scatter_rows(pick(jnp.where(to_east, second, first), one_hot, False), w["g_west"], 0)
+    scatter_rows(jnp.where(to_east, first, second), w["g_east"], -1)
+    data = (
+        lambda rows, at, l: jnp.where(to_north, got_second_h[rows, :], got_first_h[rows, :]),
+        lambda rows, at, l: jnp.where(to_north, got_first_h[rows, :], got_second_h[rows, :]),
+    )
+    sweep(data, (first_h, second_h), w)
     for c in range(COMPS):
         for l in range(LAYERS):
             w["send_east"][thickness_rows(FACE_ROWS + c * THICK, l), :] = w["load"][c * LAYERS + l]
-    to_left[...] = pick(gather_rows(w["send_west"], 0), one_hot, True)
+    west = pick(gather_rows(w["send_west"], 0), one_hot, True)
     east = gather_rows(w["send_east"], -1)
-    to_right[...] = east
+    first_c[...] = jnp.where(to_east, east, west)
+    second_c[...] = jnp.where(to_east, west, east)
     owners = owner[...]
     device = owners // PATCH_DEV
     spot = owners - device * PATCH_DEV
@@ -282,30 +345,59 @@
         term = lax.dot_general(holder, part, (((1,), (1,)), ((), ())), preferred_element_type=jnp.float32)
         total = term if total is None else total + term
     shares[...] = total
-    update(w)
+
+
+def last_kernel(got_first_c, got_second_c, got_first_h, got_second_h, match, cur, vel, inject, *refs):
+    w = dict(zip(COEFFICIENTS, refs[:5]))
+    disp_end, circ_next, height_next, ending, end_rows, turned_rows, circ_rows, sems = refs[5:]
+    w["inject"] = inject
+    to_east, to_north, _ = sides()
+    first_at = pl.multiple_of(jnp.where(to_north, FACE_ROWS, 0), 8)
+    second_at = pl.multiple_of(jnp.where(to_north, 0, FACE_ROWS), 8)
+    copies = [
+        pltpu.make_async_copy(got_first_h, height_next.at[pl.ds(first_at, FACE_ROWS)], sems.at[0]),
+        pltpu.make_async_copy(got_second_h, height_next.at[pl.ds(second_at, FACE_ROWS)], sems.at[1]),
+        pltpu.make_async_copy(end_rows, disp_end, sems.at[2]),
+        pltpu.make_async_copy(circ_rows, circ_next, sems.at[3]),
+    ]
+    copies[0].start()
+    copies[1].start()
+
+    def keep_end(h, at, values):
+        ending[h, at] = values
+
+    update(w, cur, vel, keep_end)
     for h in range(HEIGHT):
         for c in range(COMPS):
             for l in range(LAYERS):
                 rows = thickness_rows(c * THICK * HEIGHT + h, l, HEIGHT)
-                disp_end[rows, :] = roll(w["cur"][h, c * LAYERS + l], -h, 1)
-
-
-def third_kernel(from_left, from_right, south, north, match, shares, circ_next, height_next, patch_load, rows, sems):
-    copies = [
-        pltpu.make_async_copy(south, height_next.at[pl.ds(0, FACE_ROWS)], sems.at[0]),
-        pltpu.make_async_copy(north, height_next.at[pl.ds(FACE_ROWS, FACE_ROWS)], sems.at[1]),
-    ]
+                end_rows[rows, :] = roll(ending[h, c * LAYERS + l], -h, 1)
+    copies[2].start()
+    first, second = got_first_c[...], got_second_c[...]
+    west = pick(jnp.where(to_east, second, first), pairing(match), False)
+    east = jnp.where(to_east, first, second)
+    lanes = 32 * HEIGHT
+    spot = iota((FLAT, lanes), 1)
+    k, h = spot % 32, spot // 32
+    turn = jnp.where((iota((FLAT, lanes), 0) == k * HEIGHT + h) & (k < THICK), 1.0, 0.0).astype(jnp.bfloat16)
+    turned = pick(jnp.concatenate([west, east], axis=0), turn, False)
+    face = STEPS * COMPS * HEIGHT
+    for side in range(2):
+        part = turned[24 * side : 24 * (side + 1), :]
+        for h in range(HEIGHT):
+            tile = part[:, h // 4 * ARC : (h // 4 + 1) * ARC]
+            turned_rows[pl.ds(24 * HEIGHT * side + h, 24, stride=HEIGHT), :] = roll(tile, -32 * (h % 4), 1)
+        first_row = 24 * HEIGHT * side
+        circ_rows[face * side : face * (side + 1), :] = turned_rows[first_row : first_row + face, 0:THICK]
+    copies[3].start()
     for copy in copies:
-        copy.start()
-    scatter_rows(pick(from_left[...], pairing(match), False), rows, 0)
-    circ_next[0:FACE_ROWS, :] = rows[0:FACE_ROWS, 0:HEIGHT]
-    scatter_rows(from_right[...], rows, 0)
-    circ_next[FACE_ROWS : 2 * FACE_ROWS, :] = rows[0:FACE_ROWS, 0:HEIGHT]
+        copy.wait()
+
+
+def sum_kernel(shares, _, patch_load):
     total = jnp.sum(shares[...], axis=0, keepdims=True)
     for c in range(COMPS):
         patch_load[c : c + 1, :] = total[:, c * PATCH_DEV : (c + 1) * PATCH_DEV]
-    for copy in copies:
-        copy.wait()
 
 
 def f32(*shape):
@@ -315,57 +407,82 @@
 PARAMS = pltpu.CompilerParams(vmem_limit_bytes=24 * 1024 * 1024)
 VMEM = pl.BlockSpec(memory_space=pltpu.VMEM)
 ANY = pl.BlockSpec(memory_space=pl.ANY)
-
-
-def routed(to_left, to_right, to_south, to_north):
+HBM = pl.BlockSpec(memory_space=pltpu.HBM)
+
+
+def exchanged(first_c, second_c, first_h, second_h):
     blks, spans = lax.axis_size("blk"), lax.axis_size("span")
-    south = lax.ppermute(to_north, "span", [(i, i + 1) for i in range(spans - 1)])
-    north = lax.ppermute(to_south, "span", [(i + 1, i) for i in range(spans - 1)])
-    west = lax.ppermute(to_right, "blk", [(i, (i + 1) % blks) for i in range(blks)])
-    east = lax.ppermute(to_left, "blk", [((i + 1) % blks, i) for i in range(blks)])
-    return west, east, south, north
+
+    def pairs(count, start):
+        return [p for i in range(start, count, 2) for p in ((i, (i + 1) % count), ((i + 1) % count, i))]
+
+    first_h = lax.ppermute(first_h, "span", pairs(spans, 0))
+    second_h = lax.ppermute(second_h, "span", pairs(spans, 1))
+    first_c = lax.ppermute(first_c, "blk", pairs(blks, 0))
+    second_c = lax.ppermute(second_c, "blk", pairs(blks, 1))
+    return first_c, second_c, first_h, second_h
 
 
 def local(disp, velocity, modulus, guess_circ, guess_height, pair_match, patch_owner):
     disp = disp.reshape(COMPS * FLAT, ARC)
     velocity = velocity.reshape(COMPS * FLAT, ARC)
     modulus = modulus.reshape(FLAT, ARC)
-    circ = guess_circ.reshape(2 * FACE_ROWS, HEIGHT)
+    side_rows = STEPS * COMPS * HEIGHT
+    circ = jnp.swapaxes(guess_circ, 4, 5).reshape(2 * side_rows, THICK)
     rising = guess_height.reshape(2 * FACE_ROWS, ARC)
     match = pair_match.reshape(1, FLAT)
     owner = patch_owner.reshape(1, FLAT)
     face = f32(FACE_ROWS, ARC)
     flat = f32(24, FLAT)
-    sends = pl.pallas_call(
+    state = f32(*STATE_SHAPE)
+    copied = ((COMPS * FLAT, ARC), (COMPS * FLAT, ARC), (FLAT, ARC), (2 * side_rows, THICK), (2 * FACE_ROWS, ARC))
+    row = jax.ShapeDtypeStruct((1, FLAT), jnp.int32)
+    inputs = (disp, velocity, modulus, circ, rising, match, owner)
+    *sends, match, owner, cur, vel, k1, k2, k3, k4, k5 = pl.pallas_call(
         first_kernel,
-        out_shape=(flat, flat, face, face),
-        in_specs=[VMEM] * 6,
-        out_specs=(VMEM,) * 4,
-        scratch_shapes=state_shapes(),
+        out_shape=(flat, flat, face, face, row, row, state, state) + tuple(f32(*shape) for shape in COEFFICIENT_SHAPES),
+        in_specs=[HBM] * 7,
+        out_specs=(VMEM,) * 13,
+        scratch_shapes=[pltpu.VMEM(shape, jnp.float32) for shape in copied]
+        + [pltpu.SemaphoreType.DMA((7,))]
+        + [pltpu.VMEM(STATE_SHAPE, jnp.float32)] * 2
+        + work_shapes(),
         compiler_params=PARAMS,
-    )(disp, velocity, modulus, circ, rising, match)
-    west, east, south, north = routed(*sends)
-    disp_end, *sends, shares = pl.pallas_call(
+    )(*(pltpu.with_memory_space_constraint(x, pltpu.HBM) for x in inputs))
+    coefficient = (k1, k2, k3, k4, k5)
+    got = exchanged(*sends)
+    *sends, shares, inject, cur, vel = pl.pallas_call(
         second_kernel,
-        out_shape=(f32(COMPS * FLAT, ARC), flat, flat, face, face, f32(DEVICES, ARC)),
-        in_specs=[VMEM] * 9,
-        out_specs=(VMEM,) * 6,
-        scratch_shapes=state_shapes(),
+        out_shape=(flat, flat, face, face, f32(DEVICES, ARC), f32(*INJECT_SHAPE), state, state),
+        in_specs=[VMEM] * 13,
+        out_specs=(VMEM,) * 8,
+        scratch_shapes=work_shapes()[1:],
+        input_output_aliases={6: 6, 7: 7},
         compiler_params=PARAMS,
-    )(disp, velocity, modulus, west, east, south, north, match, owner)
-    west, east, south, north = routed(*sends)
+    )(*got, match, owner, cur, vel, *coefficient)
+    got = exchanged(*sends)
     shares = lax.all_to_all(shares, ("blk", "span"), split_axis=0, concat_axis=0, tiled=True)
-    circ_next, height_next, patch_load = pl.pallas_call(
-        third_kernel,
-        out_shape=(f32(2 * FACE_ROWS, HEIGHT), f32(2 * FACE_ROWS, ARC), f32(COMPS, PATCH_DEV)),
-        in_specs=[VMEM, VMEM, ANY, ANY, VMEM, VMEM],
-        out_specs=(VMEM, ANY, VMEM),
-        scratch_shapes=[pltpu.VMEM((PAD_ROWS, ARC), jnp.float32), pltpu.SemaphoreType.DMA((2,))],
+    disp_end, circ_next, height_next = pl.pallas_call(
+        last_kernel,
+        out_shape=(f32(COMPS * FLAT, ARC), f32(2 * side_rows, THICK), f32(2 * FACE_ROWS, ARC)),
+        in_specs=[VMEM, VMEM, ANY, ANY] + [VMEM] * 9,
+        out_specs=(ANY,) * 3,
+        scratch_shapes=[
+            pltpu.VMEM(STATE_SHAPE, jnp.float32),
+            pltpu.VMEM((COMPS * FLAT, ARC), jnp.float32),
+            pltpu.VMEM((2 * 24 * HEIGHT, ARC), jnp.float32),
+            pltpu.VMEM((2 * side_rows, THICK), jnp.float32),
+            pltpu.SemaphoreType.DMA((4,)),
+        ],
         compiler_params=PARAMS,
-    )(west, east, south, north, match, shares)
+    )(*got, match, cur, vel, inject, *coefficient)
+    patch_load = pl.pallas_call(
+        sum_kernel, out_shape=f32(COMPS, PATCH_DEV), in_specs=[VMEM, ANY], out_specs=VMEM, compiler_params=PARAMS
+    )(shares, pltpu.with_memory_space_constraint(circ_next, pltpu.HBM))
+    circ_next = circ_next.reshape(1, 2, STEPS, COMPS, HEIGHT, THICK)
     return (
         disp_end.reshape(COMPS, THICK, HEIGHT, ARC),
-        circ_next.reshape(1, 2, STEPS, COMPS, THICK, HEIGHT),
+        jnp.swapaxes(circ_next, 4, 5),
         height_next.reshape(1, 2, STEPS, COMPS, THICK, ARC),
         patch_load,
     )

time: 58.8 us -> 43.9 us (0.75)
  local copies, waits for them, and re-layouts: 5.79 us -> 0 us
  starting transfers between devices: 27 us -> 21.7 us
  waiting for transfers between devices: 12 us -> 8.47 us
    unnamed x14 -> x0, local copies, waits for them, and re-layouts: 5.79 us -> none
    ppermute x8, starting transfers between devices: 14.9 us -> 10.5 us  [the longest x2 3.63 us: exchanged(): second_h = lax.ppermute(second_h, 'span', pairs(spans, 1))]
    ppermute x8, waiting for transfers between devices: 7.82 us -> 5.49 us  [the longest x2 5 us: exchanged(): second_c = lax.ppermute(second_c, 'blk', pairs(blks, 1))]
    all_to_all x1, waiting for transfers between devices: 4.18 us -> 2.98 us  [local(): lax.all_to_all(shares, ('blk', 'span'), split_axis=0, concat_axis=0, tile...]
    all_to_all x1, starting transfers between devices: 12.2 us -> 11.2 us  [local(): lax.all_to_all(shares, ('blk', 'span'), split_axis=0, concat_axis=0, tile...]
    pallas_call x3 -> x4, Pallas kernels: 12.9 us -> 12.9 us  [the longest x1 5.66 us: local(): pl.pallas_call(first_kernel, out_shape=(flat, flat, face, face, row, row,...]
  transfers between devices with their start and end apart: 9 -> 9, of which waited for: 6 -> 4; matrix products, arithmetic and copies ran while one was open for 0% -> 0% of each run, Pallas kernels for 0% -> 5%
where the time goes in v2:
time: 43.9 us; the launch traced here: 43.8 us
  starting transfers between devices  21.7 us (49%)
  Pallas kernels  12.9 us (29%)
  waiting for transfers between devices  8.47 us (19%)
  between operations  0.67 us (2%)
    all_to_all x1, starting transfers between devices, local(): lax.all_to_all(shares, ('blk', 'span'), split_axis=0, concat_axis=0, tile...  11.2 us
    pallas_call x1, Pallas kernels, local(): pl.pallas_call(first_kernel, out_shape=(flat, flat, face, face, row, row,...  5.66 us
    ppermute x2, waiting for transfers between devices, exchanged(): second_c = lax.ppermute(second_c, 'blk', pairs(blks, 1))  5 us
    pallas_call x1, Pallas kernels, local(): pl.pallas_call(second_kernel, out_shape=(flat, flat, face, face, f32(DEVI...  4.58 us
    ppermute x2, starting transfers between devices, exchanged(): second_h = lax.ppermute(second_h, 'span', pairs(spans, 1))  3.63 us
    all_to_all x1, waiting for transfers between devices, local(): lax.all_to_all(shares, ('blk', 'span'), split_axis=0, concat_axis=0, tile...  2.98 us
    ppermute x2, starting transfers between devices, exchanged(): first_c = lax.ppermute(first_c, 'blk', pairs(blks, 0))  2.38 us
    ppermute x2, starting transfers between devices, exchanged(): second_c = lax.ppermute(second_c, 'blk', pairs(blks, 1))  2.36 us
  transfers between devices with their start and end apart: 9, of which 4 were waited for; matrix products, arithmetic and copies ran while one was open for 0% of the time, Pallas kernels for 5%

profile of v2, /device:TPU:1, one launch (start us, length us, event | category | flops | bytes accessed | tf_op | source)
XLA Modules:
  0.0 43.8 jit_solution(15335675968000033677)
XLA Ops:
  0.6 5.7 %shard_map.102 = (f32[24,384]{1,0:T(8,128)S(1)}, f32[24,384]{1,0:T(8,128)S(1)}, f32[432,128]{1,0:T(8,128)S(1)}, f32[432,128]{1,0:T(8,128)S(1)}, s32[1,384]{1,0:T...) custom-call(f32[1152,128]{1,0:T(8,128)} %bitcast.19, ...), custom_call_target="tpu_custom_call" | custom-call | tf_op jit(solution)/shard_map/pallas_call | solution.py:441
  6.3 2.1 %collective-permute-start.2 = (f32[432,128]{1,0:T(8,128)S(1)}, f32[432,128]{1,0:T(8,128)S(1)}, u32[]{:S(2)}, u32[]{:S(2)}) collective-permute-start(f32[432,128]{1,0:T(8,128)S(1)} %get-tuple-element.30), channel_id=1, source_target_pairs={{0,1},{1,0},{2,3},{3,2},{4,5},{5,4},{6,7},{7,6},{8,9},{9,8},{10,11... | collective-permute-start | bytes 663560 | tf_op jit(solution)/shard_map/ppermute | solution.py:419
  8.4 1.8 %collective-permute-start.3 = (f32[432,128]{1,0:T(8,128)S(1)}, f32[432,128]{1,0:T(8,128)S(1)}, u32[]{:S(2)}, u32[]{:S(2)}) collective-permute-start(f32[432,128]{1,0:T(8,128)S(1)} %get-tuple-element.31), channel_id=1, source_target_pairs={{1,2},{2,1},{3,0},{0,3},{5,6},{6,5},{7,4},{4,7},{9,10},{10,9},{11,... | collective-permute-start | bytes 663560 | tf_op jit(solution)/shard_map/ppermute | solution.py:420
  10.2 1.2 %collective-permute-start = (f32[24,384]{1,0:T(8,128)S(1)}, f32[24,384]{1,0:T(8,128)S(1)}, u32[]{:S(2)}, u32[]{:S(2)}) collective-permute-start(f32[24,384]{1,0:T(8,128)S(1)} %get-tuple-element.28), channel_id=1, source_target_pairs={{0,4},{4,0},{8,12},{12,8},{16,20},{20,16},{24,28},{28,24},{32,36},... | collective-permute-start | bytes 110600 | tf_op jit(solution)/shard_map/ppermute | solution.py:421
  11.5 1.5 %collective-permute-start.1 = (f32[24,384]{1,0:T(8,128)S(1)}, f32[24,384]{1,0:T(8,128)S(1)}, u32[]{:S(2)}, u32[]{:S(2)}) collective-permute-start(f32[24,384]{1,0:T(8,128)S(1)} %get-tuple-element.29), channel_id=1, source_target_pairs={{4,8},{8,4},{12,16},{16,12},{20,24},{24,20},{28,32},{32,28},{36,40... | collective-permute-start | bytes 110600 | tf_op jit(solution)/shard_map/ppermute | solution.py:422
  13.0 0.0 collective-permute-done.got_first_c
  13.0 2.1 %collective-permute-done.1.got_second_c = f32[24,384]{1,0:T(8,128)S(1)} collective-permute-done((f32[24,384]{1,0:T(8,128)S(1)}, f32[24,384]{1,0:T(8,128)S(1)}, u32[]{:S(2)}, u32[]{:S(2)}) %collective-permute-start.1) | collective-permute-done | bytes 36896 | tf_op jit(solution)/shard_map/ppermute | solution.py:422
  15.2 0.0 collective-permute-done.2.got_first_h
  15.2 0.5 %collective-permute-done.3.got_second_h = f32[432,128]{1,0:T(8,128)S(1)} collective-permute-done((f32[432,128]{1,0:T(8,128)S(1)}, f32[432,128]{1,0:T(8,128)S(1)}, u32[]{:S(2)}, u32[]{:S(2)}) %collective-permute-start.3) | collective-permute-done | bytes 221216 | tf_op jit(solution)/shard_map/ppermute | solution.py:420
  15.6 4.6 %shard_map.103 = (f32[24,384]{1,0:T(8,128)S(1)}, f32[24,384]{1,0:T(8,128)S(1)}, f32[432,128]{1,0:T(8,128)S(1)}, f32[432,128]{1,0:T(8,128)S(1)}, f32[128,128]{1,0...) custom-call(f32[24,384]{1,0:T(8,128)S(1)} %collective-permute-done.g, ...), custom_call_target="tpu_custom_call", output_to_operand_aliasing={{6}: (6, {}), {7}: (7, {})} | custom-call | tf_op jit(solution)/shard_map/pallas_call | solution.py:454
  20.2 0.0 collective-permute-start.6
  20.2 1.8 %collective-permute-start.7 = (f32[432,128]{1,0:T(8,128)S(1)}, f32[432,128]{1,0:T(8,128)S(1)}, u32[]{:S(2)}, u32[]{:S(2)}) collective-permute-start(f32[432,128]{1,0:T(8,128)S(1)} %get-tuple-element.44), channel_id=1, source_target_pairs={{1,2},{2,1},{3,0},{0,3},{5,6},{6,5},{7,4},{4,7},{9,10},{10,9},{11,... | collective-permute-start | bytes 663560 | tf_op jit(solution)/shard_map/ppermute | solution.py:420
  22.0 11.2 %all-to-all-start = ((f32[128,1,128]{2,1,0:T(1,128)}), f32[128,1,128]{2,1,0:T(1,128)S(1)}, u32[]{:S(2)}, u32[]{:S(2)}) async-start(f32[128,1,128]{2,1,0:T(1,128)} %bitcast.13), calls=%async_computation | async-start | bytes 131072 | tf_op jit(solution)/shard_map/all_to_all | solution.py:464
  33.2 1.1 %collective-permute-start.4 = (f32[24,384]{1,0:T(8,128)S(1)}, f32[24,384]{1,0:T(8,128)S(1)}, u32[]{:S(2)}, u32[]{:S(2)}) collective-permute-start(f32[24,384]{1,0:T(8,128)S(1)} %get-tuple-element.41), channel_id=1, source_target_pairs={{0,4},{4,0},{8,12},{12,8},{16,20},{20,16},{24,28},{28,24},{32,36},... | collective-permute-start | bytes 110600 | tf_op jit(solution)/shard_map/ppermute | solution.py:421
  34.4 0.8 %collective-permute-start.5 = (f32[24,384]{1,0:T(8,128)S(1)}, f32[24,384]{1,0:T(8,128)S(1)}, u32[]{:S(2)}, u32[]{:S(2)}) collective-permute-start(f32[24,384]{1,0:T(8,128)S(1)} %get-tuple-element.42), channel_id=1, source_target_pairs={{4,8},{8,4},{12,16},{16,12},{20,24},{24,20},{28,32},{32,28},{36,40... | collective-permute-start | bytes 110600 | tf_op jit(solution)/shard_map/ppermute | solution.py:422
  35.2 0.0 collective-permute-done.4.got_first_c
  35.2 2.8 %collective-permute-done.5.got_second_c = f32[24,384]{1,0:T(8,128)S(1)} collective-permute-done((f32[24,384]{1,0:T(8,128)S(1)}, f32[24,384]{1,0:T(8,128)S(1)}, u32[]{:S(2)}, u32[]{:S(2)}) %collective-permute-start.5) | collective-permute-done | bytes 36896 | tf_op jit(solution)/shard_map/ppermute | solution.py:422
  38.1 0.0 collective-permute-done.6.got_first_h
  38.1 0.0 collective-permute-done.7.got_second_h
  38.1 2.0 %shard_map.104 = (f32[1152,128]{1,0:T(8,128)}, f32[576,24]{1,0:T(8,128)}, f32[864,128]{1,0:T(8,128)}) custom-call(f32[24,384]{1,0:T(8,128)S(1)} %collective-permute-done.4.got_first_c, f32[24,384]{1,0:T(8,128)S(1)} %collective-permute-done.5.got_second_c, f32[432,128]{1,0:T(8,128)S(1)} %collective-permute-done.6.got_first_h, ...), custom_call_target="tpu_custom_call" | custom-call | tf_op jit(solution)/shard_map/pallas_call | solution.py:465
  40.1 3.0 %all-to-all-done = f32[128,1,128]{2,1,0:T(1,128)S(1)} async-done(((f32[128,1,128]{2,1,0:T(1,128)}), f32[128,1,128]{2,1,0:T(1,128)S(1)}, u32[]{:S(2)}, u32[]{:S(2)}) %all-to-all-start) | async-done | bytes 65568 | tf_op jit(solution)/shard_map/all_to_all | solution.py:464
  43.1 0.7 %shard_map.105 = f32[3,32]{1,0:T(4,128)} custom-call(f32[128,128]{1,0:T(8,128)S(1)} %bitcast.18, f32[576,24]{1,0:T(8,128)} %get-tuple-element.49._), custom_call_target="tpu_custom_call" | custom-call | tf_op jit(solution)/shard_map/pallas_call | solution.py:479
Async XLA Ops:
  6.3 8.9 %collective-permute-start.2 = (f32[432,128]{1,0:T(8,128)S(1)}, f32[432,128]{1,0:T(8,128)S(1)}, u32[]{:S(2)}, u32[]{:S(2)}) collective-permute-start(f32[432,128]{1,0:T(8,128)S(1)} %get-tuple-element.30), channel_id=1, source_target_pairs={{0,1},{1,0},{2,3},{3,2},{4,5},{5,4},{6,7},{7,6},{8,9},{9,8},{10,11... | collective-permute-start | bytes 663560 | tf_op jit(solution)/shard_map/ppermute | solution.py:419
  8.4 7.2 %collective-permute-start.3 = (f32[432,128]{1,0:T(8,128)S(1)}, f32[432,128]{1,0:T(8,128)S(1)}, u32[]{:S(2)}, u32[]{:S(2)}) collective-permute-start(f32[432,128]{1,0:T(8,128)S(1)} %get-tuple-element.31), channel_id=1, source_target_pairs={{1,2},{2,1},{3,0},{0,3},{5,6},{6,5},{7,4},{4,7},{9,10},{10,9},{11,... | collective-permute-start | bytes 663560 | tf_op jit(solution)/shard_map/ppermute | solution.py:420
  10.2 2.8 %collective-permute-start = (f32[24,384]{1,0:T(8,128)S(1)}, f32[24,384]{1,0:T(8,128)S(1)}, u32[]{:S(2)}, u32[]{:S(2)}) collective-permute-start(f32[24,384]{1,0:T(8,128)S(1)} %get-tuple-element.28), channel_id=1, source_target_pairs={{0,4},{4,0},{8,12},{12,8},{16,20},{20,16},{24,28},{28,24},{32,36},... | collective-permute-start | bytes 110600 | tf_op jit(solution)/shard_map/ppermute | solution.py:421
  11.5 3.7 %collective-permute-start.1 = (f32[24,384]{1,0:T(8,128)S(1)}, f32[24,384]{1,0:T(8,128)S(1)}, u32[]{:S(2)}, u32[]{:S(2)}) collective-permute-start(f32[24,384]{1,0:T(8,128)S(1)} %get-tuple-element.29), channel_id=1, source_target_pairs={{4,8},{8,4},{12,16},{16,12},{20,24},{24,20},{28,32},{32,28},{36,40... | collective-permute-start | bytes 110600 | tf_op jit(solution)/shard_map/ppermute | solution.py:422
  20.2 17.9 %collective-permute-start.6 = (f32[432,128]{1,0:T(8,128)S(1)}, f32[432,128]{1,0:T(8,128)S(1)}, u32[]{:S(2)}, u32[]{:S(2)}) collective-permute-start(f32[432,128]{1,0:T(8,128)S(1)} %get-tuple-element.43), channel_id=1, source_target_pairs={{0,1},{1,0},{2,3},{3,2},{4,5},{5,4},{6,7},{7,6},{8,9},{9,8},{10,11... | collective-permute-start | bytes 663560 | tf_op jit(solution)/shard_map/ppermute | solution.py:419
  20.2 17.9 %collective-permute-start.7 = (f32[432,128]{1,0:T(8,128)S(1)}, f32[432,128]{1,0:T(8,128)S(1)}, u32[]{:S(2)}, u32[]{:S(2)}) collective-permute-start(f32[432,128]{1,0:T(8,128)S(1)} %get-tuple-element.44), channel_id=1, source_target_pairs={{1,2},{2,1},{3,0},{0,3},{5,6},{6,5},{7,4},{4,7},{9,10},{10,9},{11,... | collective-permute-start | bytes 663560 | tf_op jit(solution)/shard_map/ppermute | solution.py:420
  22.0 21.1 %all-to-all-start = ((f32[128,1,128]{2,1,0:T(1,128)}), f32[128,1,128]{2,1,0:T(1,128)S(1)}, u32[]{:S(2)}, u32[]{:S(2)}) async-start(f32[128,1,128]{2,1,0:T(1,128)} %bitcast.13), calls=%async_computation | async-start | bytes 131072 | tf_op jit(solution)/shard_map/all_to_all | solution.py:464
  33.2 2.0 %collective-permute-start.4 = (f32[24,384]{1,0:T(8,128)S(1)}, f32[24,384]{1,0:T(8,128)S(1)}, u32[]{:S(2)}, u32[]{:S(2)}) collective-permute-start(f32[24,384]{1,0:T(8,128)S(1)} %get-tuple-element.41), channel_id=1, source_target_pairs={{0,4},{4,0},{8,12},{12,8},{16,20},{20,16},{24,28},{28,24},{32,36},... | collective-permute-start | bytes 110600 | tf_op jit(solution)/shard_map/ppermute | solution.py:421
  34.4 3.7 %collective-permute-start.5 = (f32[24,384]{1,0:T(8,128)S(1)}, f32[24,384]{1,0:T(8,128)S(1)}, u32[]{:S(2)}, u32[]{:S(2)}) collective-permute-start(f32[24,384]{1,0:T(8,128)S(1)} %get-tuple-element.42), channel_id=1, source_target_pairs={{4,8},{8,4},{12,16},{16,12},{20,24},{24,20},{28,32},{32,28},{36,40... | collective-permute-start | bytes 110600 | tf_op jit(solution)/shard_map/ppermute | solution.py:422

commit v3 on v2

--- a/solution.py
+++ b/solution.py
@@ -96,52 +96,70 @@
     return east, north, inner
 
 
-def record(step, data, sends, w):
+def face_rates(w):
+    lane = iota((8, ARC), 1)
+    zero = jnp.zeros((8, ARC), jnp.float32)
+
+    def rates(c, l):
+        b = c * LAYERS + l
+        west, east = zero, zero
+        for h in range(HEIGHT):
+            v = w["vel"][h, b]
+            west = jnp.where(lane == h, v, west)
+            east = jnp.where(lane == (h - 1) % ARC, v, east)
+        north = roll(w["faces"][3, l] * w["vel"][HEIGHT - 1, b], 1 - HEIGHT, 1)
+        return w["faces"][0, l] * west, w["faces"][1, l] * east, w["faces"][2, l] * w["vel"][0, b], north
+
+    return rates
+
+
+def record(step, rates, data, sends, w):
     south_of, north_of = data
     send_first, send_second = sends
     _, to_north, inner = sides()
     weight = jnp.where(inner, 1.0, 0.0)
-    lane = iota((8, ARC), 1)
-    zero = jnp.zeros((8, ARC), jnp.float32)
     for c in range(COMPS):
         for l in range(LAYERS):
             b = c * LAYERS + l
-            west, east = zero, zero
-            for h in range(HEIGHT):
-                v = w["vel"][h, b]
-                west = jnp.where(lane == h, v, west)
-                east = jnp.where(lane == (h - 1) % ARC, v, east)
+            rate_west, rate_east, rate_south, rate_north = rates(c, l)
             rows = thickness_rows(step * (COMPS * THICK) + c * THICK, l)
             g = w["g_west"][rows, :]
             w["inject"][0, b] = 0.04 * g
-            w["send_west"][rows, :] = 2.0 * (w["faces"][0, l] * west) - g
+            w["send_west"][rows, :] = 2.0 * rate_west - g
             g = w["g_east"][rows, :]
             w["inject"][1, b] = 0.04 * g
-            rate = w["faces"][1, l] * east
-            w["send_east"][rows, :] = 2.0 * rate - g
-            w["load"][b] = w["load"][b] + (g - rate)
+            w["send_east"][rows, :] = 2.0 * rate_east - g
+            w["load"][b] = w["load"][b] + (g - rate_east)
             g = south_of(rows, step * (COMPS * THICK) + c * THICK, l)
             w["inject"][2, b] = 0.04 * g
-            south = 2.0 * (w["faces"][2, l] * w["vel"][0, b]) - g
+            south = 2.0 * rate_south - g
             g = north_of(rows, step * (COMPS * THICK) + c * THICK, l)
             w["inject"][3, b] = roll(0.04 * g, HEIGHT - 1, 1)
-            rate = w["faces"][3, l] * w["vel"][HEIGHT - 1, b]
-            north = roll(2.0 * rate, 1 - HEIGHT, 1) - g
+            north = 2.0 * rate_north - g
             send_first[rows, :] = jnp.where(to_north, north, south)
             send_second[rows, :] = weight * jnp.where(to_north, south, north)
 
 
-def update(w, from_cur=None, from_vel=None, sink=None):
+def injected(h, at, w):
+    lane = iota((8, ARC), 1)
+    on_west = lane == h
+    on_edge = on_west | (lane == (h - 1) % ARC)
+    g = jnp.where(on_edge, jnp.where(on_west, w["inject"][0, at], w["inject"][1, at]), 0.0)
+    if h == 0:
+        g = g + w["inject"][2, at]
+    if h == HEIGHT - 1:
+        g = g + w["inject"][3, at]
+    return g
+
+
+def update(w, from_cur=None, from_vel=None, sink=None, inject=True):
     from_cur = w["cur"] if from_cur is None else from_cur
     from_vel = w["vel"] if from_vel is None else from_vel
-    lane = iota((8, ARC), 1)
     blocks = [(c, l) for c in range(COMPS) for l in range(LAYERS)]
     cur = {b: from_cur[0, b[0] * LAYERS + b[1]] for b in blocks}
     left = {b: roll(cur[b], -1, 1) for b in blocks}
     rising = {}
     for h in range(HEIGHT):
-        on_west = lane == h
-        on_edge = on_west | (lane == (h - 1) % ARC)
         last = h + 1 == HEIGHT
         cur_next, left_next = {}, {}
         for c in range(COMPS):
@@ -165,12 +183,8 @@
                     left_next[b] = roll(cur_next[b], -1, 1)
                     rising[b] = w["along_h"][h, l] * (left_next[b] - here)
                     total = total + rising[b]
-                g = jnp.where(on_west, w["inject"][0, at], w["inject"][1, at])
-                total = total + jnp.where(on_edge, g, 0.0)
-                if h == 0:
-                    total = total + w["inject"][2, at]
-                if last:
-                    total = total + w["inject"][3, at]
+                if inject:
+                    total = total + injected(h, at, w)
                 v = w["keep"][h, l] * from_vel[h, at] + total
                 if sink is None:
                     w["vel"][h, at] = v
@@ -220,16 +234,14 @@
     return jnp.where(iota((FLAT, FLAT), 0) == match[...], 1.0, 0.0).astype(jnp.bfloat16)
 
 
-def sweep(data, sends, w):
-    w["load"][...] = jnp.zeros_like(w["load"])
-
+def sweep(first_step, data, sends, w):
     def one(step, carry):
-        record(step, data, sends, w)
+        record(step, face_rates(w), data, sends, w)
         update(w)
         return carry
 
-    lax.fori_loop(0, STEPS - 1, one, 0)
-    record(STEPS - 1, data, sends, w)
+    lax.fori_loop(first_step, STEPS - 1, one, 0)
+    record(STEPS - 1, face_rates(w), data, sends, w)
 
 
 WORK = ("inject", "load", "g_west", "g_east", "send_west", "send_east")
@@ -301,7 +313,8 @@
         lambda rows, at, l: rising_in[thickness_rows(at, l), :],
         lambda rows, at, l: rising_in[thickness_rows(FACE_ROWS + at, l), :],
     )
-    sweep(data, (first_h, second_h), w)
+    w["load"][...] = jnp.zeros_like(w["load"])
+    sweep(0, data, (first_h, second_h), w)
     west = pick(gather_rows(w["send_west"], 0), pairing(match), True)
     east = gather_rows(w["send_east"], -1)
     to_east, _, _ = sides()
@@ -309,12 +322,24 @@
     second_c[...] = jnp.where(to_east, west, east)
 
 
-def second_kernel(got_first_c, got_second_c, got_first_h, got_second_h, match, owner, cur0, vel0, *refs):
+def middle_kernel(match, cur0, vel0, *refs):
+    w = dict(zip(COEFFICIENTS, refs[:5]))
+    rates, one_hot, w["cur"], w["vel"] = refs[5:]
+    one_hot[...] = pairing(match)
+    of = face_rates(w)
+    for c in range(COMPS):
+        for l in range(LAYERS):
+            for side, values in enumerate(of(c, l)):
+                rates[side, c * LAYERS + l] = values
+    update(w, inject=False)
+
+
+def second_kernel(got_first_c, got_second_c, got_first_h, got_second_h, pairs, rates, owner, cur1, vel1, *refs):
     w = dict(zip(COEFFICIENTS, refs[:5]))
     first_c, second_c, first_h, second_h, shares, inject, w["cur"], w["vel"] = refs[5:13]
     w.update(zip(WORK, (inject,) + refs[13:]))
     clear_tail(w)
-    one_hot = pairing(match)
+    one_hot = pairs[...]
     to_east, to_north, _ = sides()
     first, second = got_first_c[...], got_second_c[...]
     scatter_rows(pick(jnp.where(to_east, second, first), one_hot, False), w["g_west"], 0)
@@ -323,7 +348,14 @@
         lambda rows, at, l: jnp.where(to_north, got_second_h[rows, :], got_first_h[rows, :]),
         lambda rows, at, l: jnp.where(to_north, got_first_h[rows, :], got_second_h[rows, :]),
     )
-    sweep(data, (first_h, second_h), w)
+    w["load"][...] = jnp.zeros_like(w["load"])
+    record(0, lambda c, l: [rates[side, c * LAYERS + l] for side in range(4)], data, (first_h, second_h), w)
+    for h in range(HEIGHT):
+        for at in range(COMPS * LAYERS):
+            g = injected(h, at, w)
+            w["vel"][h, at] = w["vel"][h, at] + g
+            w["cur"][h, at] = w["cur"][h, at] + g
+    sweep(1, data, (first_h, second_h), w)
     for c in range(COMPS):
         for l in range(LAYERS):
             w["send_east"][thickness_rows(FACE_ROWS + c * THICK, l), :] = w["load"][c * LAYERS + l]
@@ -347,32 +379,33 @@
     shares[...] = total
 
 
-def last_kernel(got_first_c, got_second_c, got_first_h, got_second_h, match, cur, vel, inject, *refs):
+def end_kernel(cur, vel, inject, *refs):
     w = dict(zip(COEFFICIENTS, refs[:5]))
-    disp_end, circ_next, height_next, ending, end_rows, turned_rows, circ_rows, sems = refs[5:]
+    disp_end, ending = refs[5:]
     w["inject"] = inject
+
+    def keep_end(h, at, values):
+        ending[h, at] = values
+
+    update(w, cur, vel, keep_end)
+    for h in range(HEIGHT):
+        for c in range(COMPS):
+            for l in range(LAYERS):
+                rows = thickness_rows(c * THICK * HEIGHT + h, l, HEIGHT)
+                disp_end[rows, :] = roll(ending[h, c * LAYERS + l], -h, 1)
+
+
+def face_kernel(got_first_c, got_second_c, got_first_h, got_second_h, match, _, *refs):
+    circ_next, height_next, turned_rows, sems = refs
     to_east, to_north, _ = sides()
     first_at = pl.multiple_of(jnp.where(to_north, FACE_ROWS, 0), 8)
     second_at = pl.multiple_of(jnp.where(to_north, 0, FACE_ROWS), 8)
     copies = [
         pltpu.make_async_copy(got_first_h, height_next.at[pl.ds(first_at, FACE_ROWS)], sems.at[0]),
         pltpu.make_async_copy(got_second_h, height_next.at[pl.ds(second_at, FACE_ROWS)], sems.at[1]),
-        pltpu.make_async_copy(end_rows, disp_end, sems.at[2]),
-        pltpu.make_async_copy(circ_rows, circ_next, sems.at[3]),
     ]
-    copies[0].start()
-    copies[1].start()
-
-    def keep_end(h, at, values):
-        ending[h, at] = values
-
-    update(w, cur, vel, keep_end)
-    for h in range(HEIGHT):
-        for c in range(COMPS):
-            for l in range(LAYERS):
-                rows = thickness_rows(c * THICK * HEIGHT + h, l, HEIGHT)
-                end_rows[rows, :] = roll(ending[h, c * LAYERS + l], -h, 1)
-    copies[2].start()
+    for copy in copies:
+        copy.start()
     first, second = got_first_c[...], got_second_c[...]
     west = pick(jnp.where(to_east, second, first), pairing(match), False)
     east = jnp.where(to_east, first, second)
@@ -388,8 +421,7 @@
             tile = part[:, h // 4 * ARC : (h // 4 + 1) * ARC]
             turned_rows[pl.ds(24 * HEIGHT * side + h, 24, stride=HEIGHT), :] = roll(tile, -32 * (h % 4), 1)
         first_row = 24 * HEIGHT * side
-        circ_rows[face * side : face * (side + 1), :] = turned_rows[first_row : first_row + face, 0:THICK]
-    copies[3].start()
+        circ_next[face * side : face * (side + 1), :] = turned_rows[first_row : first_row + face, 0:THICK]
     for copy in copies:
         copy.wait()
 
@@ -451,31 +483,42 @@
     )(*(pltpu.with_memory_space_constraint(x, pltpu.HBM) for x in inputs))
     coefficient = (k1, k2, k3, k4, k5)
     got = exchanged(*sends)
+    rates, pairs, cur, vel = pl.pallas_call(
+        middle_kernel,
+        out_shape=(f32(*INJECT_SHAPE), jax.ShapeDtypeStruct((FLAT, FLAT), jnp.bfloat16), state, state),
+        in_specs=[VMEM] * 8,
+        out_specs=(VMEM,) * 4,
+        input_output_aliases={1: 2, 2: 3},
+        compiler_params=PARAMS,
+        cost_estimate=pl.CostEstimate(flops=3 * 10**6, bytes_accessed=4 * 10**6, transcendentals=0),
+    )(match, cur, vel, *coefficient)
     *sends, shares, inject, cur, vel = pl.pallas_call(
         second_kernel,
         out_shape=(flat, flat, face, face, f32(DEVICES, ARC), f32(*INJECT_SHAPE), state, state),
-        in_specs=[VMEM] * 13,
+        in_specs=[VMEM] * 14,
         out_specs=(VMEM,) * 8,
         scratch_shapes=work_shapes()[1:],
-        input_output_aliases={6: 6, 7: 7},
+        input_output_aliases={7: 6, 8: 7},
         compiler_params=PARAMS,
-    )(*got, match, owner, cur, vel, *coefficient)
+    )(*got, pairs, rates, owner, cur, vel, *coefficient)
     got = exchanged(*sends)
     shares = lax.all_to_all(shares, ("blk", "span"), split_axis=0, concat_axis=0, tiled=True)
-    disp_end, circ_next, height_next = pl.pallas_call(
-        last_kernel,
-        out_shape=(f32(COMPS * FLAT, ARC), f32(2 * side_rows, THICK), f32(2 * FACE_ROWS, ARC)),
-        in_specs=[VMEM, VMEM, ANY, ANY] + [VMEM] * 9,
-        out_specs=(ANY,) * 3,
-        scratch_shapes=[
-            pltpu.VMEM(STATE_SHAPE, jnp.float32),
-            pltpu.VMEM((COMPS * FLAT, ARC), jnp.float32),
-            pltpu.VMEM((2 * 24 * HEIGHT, ARC), jnp.float32),
-            pltpu.VMEM((2 * side_rows, THICK), jnp.float32),
-            pltpu.SemaphoreType.DMA((4,)),
-        ],
+    disp_end = pl.pallas_call(
+        end_kernel,
+        out_shape=f32(COMPS * FLAT, ARC),
+        in_specs=[VMEM] * 8,
+        out_specs=VMEM,
+        scratch_shapes=[pltpu.VMEM(STATE_SHAPE, jnp.float32)],
         compiler_params=PARAMS,
-    )(*got, match, cur, vel, inject, *coefficient)
+    )(cur, vel, inject, *coefficient)
+    circ_next, height_next = pl.pallas_call(
+        face_kernel,
+        out_shape=(f32(2 * side_rows, THICK), f32(2 * FACE_ROWS, ARC)),
+        in_specs=[VMEM, VMEM, ANY, ANY, VMEM, ANY],
+        out_specs=(VMEM, ANY),
+        scratch_shapes=[pltpu.VMEM((2 * 24 * HEIGHT, ARC), jnp.float32), pltpu.SemaphoreType.DMA((2,))],
+        compiler_params=PARAMS,
+    )(*got, match, pltpu.with_memory_space_constraint(disp_end, pltpu.HBM))
     patch_load = pl.pallas_call(
         sum_kernel, out_shape=f32(COMPS, PATCH_DEV), in_specs=[VMEM, ANY], out_specs=VMEM, compiler_params=PARAMS
     )(shares, pltpu.with_memory_space_constraint(circ_next, pltpu.HBM))

time: 43.9 us -> 43.3 us (0.986)
  waiting for transfers between devices: 8.47 us -> 6.6 us
  Pallas kernels: 12.9 us -> 14.1 us
    ppermute x2, waiting for transfers between devices: 5 us -> 2.69 us  [exchanged(): second_c = lax.ppermute(second_c, 'blk', pairs(blks, 1))]
    pallas_call x1 -> x3, Pallas kernels: 2.03 us -> 3.89 us  [the longest x1 1.63 us: local(): pl.pallas_call(end_kernel, out_shape=f32(COMPS * FLAT, ARC), in_specs=[VM...]
    pallas_call x1, Pallas kernels: 4.58 us -> 4.05 us  [local(): pl.pallas_call(second_kernel, out_shape=(flat, flat, face, face, f32(DEVI...]
    all_to_all x1, waiting for transfers between devices: 2.98 us -> 3.45 us  [local(): lax.all_to_all(shares, ('blk', 'span'), split_axis=0, concat_axis=0, tile...]
  transfers between devices with their start and end apart: 9 -> 9, of which waited for: 4 -> 4; matrix products, arithmetic and copies ran while one was open for 0% -> 0% of each run, Pallas kernels for 5% -> 9%
where the time goes in v3:
time: 43.3 us; the launch traced here: 43.1 us
  starting transfers between devices  21.7 us (50%)
  Pallas kernels  14.1 us (33%)
  waiting for transfers between devices  6.6 us (15%)
  between operations  0.68 us (2%)
    all_to_all x1, starting transfers between devices, local(): lax.all_to_all(shares, ('blk', 'span'), split_axis=0, concat_axis=0, tile...  11.2 us
    pallas_call x1, Pallas kernels, local(): pl.pallas_call(first_kernel, out_shape=(flat, flat, face, face, row, row,...  5.55 us
    pallas_call x1, Pallas kernels, local(): pl.pallas_call(second_kernel, out_shape=(flat, flat, face, face, f32(DEVI...  4.05 us
    ppermute x2, starting transfers between devices, exchanged(): second_h = lax.ppermute(second_h, 'span', pairs(spans, 1))  3.63 us
    all_to_all x1, waiting for transfers between devices, local(): lax.all_to_all(shares, ('blk', 'span'), split_axis=0, concat_axis=0, tile...  3.45 us
    ppermute x2, waiting for transfers between devices, exchanged(): second_c = lax.ppermute(second_c, 'blk', pairs(blks, 1))  2.69 us
    ppermute x2, starting transfers between devices, exchanged(): first_c = lax.ppermute(first_c, 'blk', pairs(blks, 0))  2.38 us
    ppermute x2, starting transfers between devices, exchanged(): second_c = lax.ppermute(second_c, 'blk', pairs(blks, 1))  2.36 us
  transfers between devices with their start and end apart: 9, of which 4 were waited for; matrix products, arithmetic and copies ran while one was open for 0% of the time, Pallas kernels for 9%

profile of v3, /device:TPU:1, one launch (start us, length us, event | category | flops | bytes accessed | tf_op | source)
XLA Modules:
  0.0 43.1 jit_solution(17759844574407570121)
XLA Ops:
  0.6 5.5 %shard_map.102 = (f32[24,384]{1,0:T(8,128)S(1)}, f32[24,384]{1,0:T(8,128)S(1)}, f32[432,128]{1,0:T(8,128)S(1)}, f32[432,128]{1,0:T(8,128)S(1)}, s32[1,384]{1,0:T...) custom-call(f32[1152,128]{1,0:T(8,128)} %bitcast.20, ...), custom_call_target="tpu_custom_call" | custom-call | tf_op jit(solution)/shard_map/pallas_call | solution.py:473
  6.2 2.1 %collective-permute-start.2 = (f32[432,128]{1,0:T(8,128)S(1)}, f32[432,128]{1,0:T(8,128)S(1)}, u32[]{:S(2)}, u32[]{:S(2)}) collective-permute-start(f32[432,128]{1,0:T(8,128)S(1)} %get-tuple-element.33), channel_id=1, source_target_pairs={{0,1},{1,0},{2,3},{3,2},{4,5},{5,4},{6,7},{7,6},{8,9},{9,8},{10,11... | collective-permute-start | bytes 663560 | tf_op jit(solution)/shard_map/ppermute | solution.py:451
  8.3 1.8 %collective-permute-start.3 = (f32[432,128]{1,0:T(8,128)S(1)}, f32[432,128]{1,0:T(8,128)S(1)}, u32[]{:S(2)}, u32[]{:S(2)}) collective-permute-start(f32[432,128]{1,0:T(8,128)S(1)} %get-tuple-element.34), channel_id=1, source_target_pairs={{1,2},{2,1},{3,0},{0,3},{5,6},{6,5},{7,4},{4,7},{9,10},{10,9},{11,... | collective-permute-start | bytes 663560 | tf_op jit(solution)/shard_map/ppermute | solution.py:452
  10.1 1.2 %collective-permute-start = (f32[24,384]{1,0:T(8,128)S(1)}, f32[24,384]{1,0:T(8,128)S(1)}, u32[]{:S(2)}, u32[]{:S(2)}) collective-permute-start(f32[24,384]{1,0:T(8,128)S(1)} %get-tuple-element.31), channel_id=1, source_target_pairs={{0,4},{4,0},{8,12},{12,8},{16,20},{20,16},{24,28},{28,24},{32,36},... | collective-permute-start | bytes 110600 | tf_op jit(solution)/shard_map/ppermute | solution.py:453
  11.4 1.5 %collective-permute-start.1 = (f32[24,384]{1,0:T(8,128)S(1)}, f32[24,384]{1,0:T(8,128)S(1)}, u32[]{:S(2)}, u32[]{:S(2)}) collective-permute-start(f32[24,384]{1,0:T(8,128)S(1)} %get-tuple-element.32), channel_id=1, source_target_pairs={{4,8},{8,4},{12,16},{16,12},{20,24},{24,20},{28,32},{32,28},{36,40... | collective-permute-start | bytes 110600 | tf_op jit(solution)/shard_map/ppermute | solution.py:454
  12.9 0.7 %shard_map.103 = (f32[4,9,8,128]{3,2,1,0:T(8,128)S(1)}, bf16[384,384]{1,0:T(8,128)(2,1)S(1)}, f32[16,9,8,128]{3,2,1,0:T(8,128)S(1)}, f32[16,9,8,128]{3,2,1,0:T(8,128)S(1)}) custom-call(s32[1,384]{1,0:T(1,128)S(1)} %get-tuple-element.35.match, f32[16,9,8,128]{3,2,1,0:T(8,128)S(1)} %get-tuple-element.36.cur0, ...), custom_call_target="tpu_custom_call", output_to_operand_aliasing={{2}: (1, {}), {3}: (2, {})} | custom-call | flops 3000000 | bytes 4000000 | tf_op jit(solution)/shard_map/pallas_call | solution.py:486
  13.6 0.0 collective-permute-done.got_first_c
  13.6 1.4 %collective-permute-done.1.got_second_c = f32[24,384]{1,0:T(8,128)S(1)} collective-permute-done((f32[24,384]{1,0:T(8,128)S(1)}, f32[24,384]{1,0:T(8,128)S(1)}, u32[]{:S(2)}, u32[]{:S(2)}) %collective-permute-start.1) | collective-permute-done | bytes 36896 | tf_op jit(solution)/shard_map/ppermute | solution.py:454
  15.0 0.0 collective-permute-done.2.got_first_h
  15.0 0.5 %collective-permute-done.3.got_second_h = f32[432,128]{1,0:T(8,128)S(1)} collective-permute-done((f32[432,128]{1,0:T(8,128)S(1)}, f32[432,128]{1,0:T(8,128)S(1)}, u32[]{:S(2)}, u32[]{:S(2)}) %collective-permute-start.3) | collective-permute-done | bytes 221216 | tf_op jit(solution)/shard_map/ppermute | solution.py:452
  15.5 4.0 %shard_map.104 = (f32[24,384]{1,0:T(8,128)S(1)}, f32[24,384]{1,0:T(8,128)S(1)}, f32[432,128]{1,0:T(8,128)S(1)}, f32[432,128]{1,0:T(8,128)S(1)}, f32[128,128]{1,0...) custom-call(f32[24,384]{1,0:T(8,128)S(1)} %collective-permute-done.g, ...), custom_call_target="tpu_custom_call", output_to_operand_aliasing={{6}: (7, {}), {7}: (8, {})} | custom-call | tf_op jit(solution)/shard_map/pallas_call | solution.py:495
  19.5 0.0 collective-permute-start.6
  19.5 1.8 %collective-permute-start.7 = (f32[432,128]{1,0:T(8,128)S(1)}, f32[432,128]{1,0:T(8,128)S(1)}, u32[]{:S(2)}, u32[]{:S(2)}) collective-permute-start(f32[432,128]{1,0:T(8,128)S(1)} %get-tuple-element.54), channel_id=1, source_target_pairs={{1,2},{2,1},{3,0},{0,3},{5,6},{6,5},{7,4},{4,7},{9,10},{10,9},{11,... | collective-permute-start | bytes 663560 | tf_op jit(solution)/shard_map/ppermute | solution.py:452
  21.4 11.2 %all-to-all-start = ((f32[128,1,128]{2,1,0:T(1,128)}), f32[128,1,128]{2,1,0:T(1,128)S(1)}, u32[]{:S(2)}, u32[]{:S(2)}) async-start(f32[128,1,128]{2,1,0:T(1,128)} %bitcast.13), calls=%async_computation | async-start | bytes 131072 | tf_op jit(solution)/shard_map/all_to_all | solution.py:505
  32.6 1.1 %collective-permute-start.4 = (f32[24,384]{1,0:T(8,128)S(1)}, f32[24,384]{1,0:T(8,128)S(1)}, u32[]{:S(2)}, u32[]{:S(2)}) collective-permute-start(f32[24,384]{1,0:T(8,128)S(1)} %get-tuple-element.51), channel_id=1, source_target_pairs={{0,4},{4,0},{8,12},{12,8},{16,20},{20,16},{24,28},{28,24},{32,36},... | collective-permute-start | bytes 110600 | tf_op jit(solution)/shard_map/ppermute | solution.py:453
  33.7 0.8 %collective-permute-start.5 = (f32[24,384]{1,0:T(8,128)S(1)}, f32[24,384]{1,0:T(8,128)S(1)}, u32[]{:S(2)}, u32[]{:S(2)}) collective-permute-start(f32[24,384]{1,0:T(8,128)S(1)} %get-tuple-element.52), channel_id=1, source_target_pairs={{4,8},{8,4},{12,16},{16,12},{20,24},{24,20},{28,32},{32,28},{36,40... | collective-permute-start | bytes 110600 | tf_op jit(solution)/shard_map/ppermute | solution.py:454
  34.5 1.6 %shard_map.105._ = f32[1152,128]{1,0:T(8,128)} custom-call(f32[16,9,8,128]{3,2,1,0:T(8,128)S(1)} %get-tuple-element.48.cur, f32[16,9,8,128]{3,2,1,0:T(8,128)S(1)} %get-tuple-element.49.vel, f32[4,9,8,128]{3,2,1,0:T(8,128)S(1)} %get-tuple-element.50.inject, f32[16,3,8,128]{3,2,1,0:T(8,128)S(1)} %get-tuple-element.38.refs_0_, ...), custom_call_target="tpu_custom_call" | custom-call | tf_op jit(solution)/shard_map/pallas_call | solution.py:506
  36.2 0.0 collective-permute-done.4.got_first_c
  36.2 1.3 %collective-permute-done.5.got_second_c = f32[24,384]{1,0:T(8,128)S(1)} collective-permute-done((f32[24,384]{1,0:T(8,128)S(1)}, f32[24,384]{1,0:T(8,128)S(1)}, u32[]{:S(2)}, u32[]{:S(2)}) %collective-permute-start.5) | collective-permute-done | bytes 36896 | tf_op jit(solution)/shard_map/ppermute | solution.py:454
  37.4 0.0 collective-permute-done.6.got_first_h
  37.4 0.0 collective-permute-done.7.got_second_h
  37.4 1.5 %shard_map.106 = (f32[576,24]{1,0:T(8,128)}, f32[864,128]{1,0:T(8,128)}) custom-call(f32[24,384]{1,0:T(8,128)S(1)} %collective-permute-done.4.got_first_c, f32[24,384]{1,0:T(8,128)S(1)} %collective-permute-done.5.got_second_c, f32[432,128]{1,0:T(8,128)S(1)} %collective-permute-done.6.got_first_h, f32[432,128]{1,0:T(8,128)S(1)} %collective-permute-done.7.got_second_h, ...), custom_call_target="tpu_custom_call" | custom-call | tf_op jit(solution)/shard_map/pallas_call | solution.py:514
  39.0 3.4 %all-to-all-done = f32[128,1,128]{2,1,0:T(1,128)S(1)} async-done(((f32[128,1,128]{2,1,0:T(1,128)}), f32[128,1,128]{2,1,0:T(1,128)S(1)}, u32[]{:S(2)}, u32[]{:S(2)}) %all-to-all-start) | async-done | bytes 65568 | tf_op jit(solution)/shard_map/all_to_all | solution.py:505
  42.4 0.7 %shard_map.107 = f32[3,32]{1,0:T(4,128)} custom-call(f32[128,128]{1,0:T(8,128)S(1)} %bitcast.18, f32[576,24]{1,0:T(8,128)} %get-tuple-element.55._), custom_call_target="tpu_custom_call" | custom-call | tf_op jit(solution)/shard_map/pallas_call | solution.py:522
Async XLA Ops:
  6.2 8.9 %collective-permute-start.2 = (f32[432,128]{1,0:T(8,128)S(1)}, f32[432,128]{1,0:T(8,128)S(1)}, u32[]{:S(2)}, u32[]{:S(2)}) collective-permute-start(f32[432,128]{1,0:T(8,128)S(1)} %get-tuple-element.33), channel_id=1, source_target_pairs={{0,1},{1,0},{2,3},{3,2},{4,5},{5,4},{6,7},{7,6},{8,9},{9,8},{10,11... | collective-permute-start | bytes 663560 | tf_op jit(solution)/shard_map/ppermute | solution.py:451
  8.3 7.2 %collective-permute-start.3 = (f32[432,128]{1,0:T(8,128)S(1)}, f32[432,128]{1,0:T(8,128)S(1)}, u32[]{:S(2)}, u32[]{:S(2)}) collective-permute-start(f32[432,128]{1,0:T(8,128)S(1)} %get-tuple-element.34), channel_id=1, source_target_pairs={{1,2},{2,1},{3,0},{0,3},{5,6},{6,5},{7,4},{4,7},{9,10},{10,9},{11,... | collective-permute-start | bytes 663560 | tf_op jit(solution)/shard_map/ppermute | solution.py:452
  10.1 3.5 %collective-permute-start = (f32[24,384]{1,0:T(8,128)S(1)}, f32[24,384]{1,0:T(8,128)S(1)}, u32[]{:S(2)}, u32[]{:S(2)}) collective-permute-start(f32[24,384]{1,0:T(8,128)S(1)} %get-tuple-element.31), channel_id=1, source_target_pairs={{0,4},{4,0},{8,12},{12,8},{16,20},{20,16},{24,28},{28,24},{32,36},... | collective-permute-start | bytes 110600 | tf_op jit(solution)/shard_map/ppermute | solution.py:453
  11.4 3.7 %collective-permute-start.1 = (f32[24,384]{1,0:T(8,128)S(1)}, f32[24,384]{1,0:T(8,128)S(1)}, u32[]{:S(2)}, u32[]{:S(2)}) collective-permute-start(f32[24,384]{1,0:T(8,128)S(1)} %get-tuple-element.32), channel_id=1, source_target_pairs={{4,8},{8,4},{12,16},{16,12},{20,24},{24,20},{28,32},{32,28},{36,40... | collective-permute-start | bytes 110600 | tf_op jit(solution)/shard_map/ppermute | solution.py:454
  19.5 17.9 %collective-permute-start.6 = (f32[432,128]{1,0:T(8,128)S(1)}, f32[432,128]{1,0:T(8,128)S(1)}, u32[]{:S(2)}, u32[]{:S(2)}) collective-permute-start(f32[432,128]{1,0:T(8,128)S(1)} %get-tuple-element.53), channel_id=1, source_target_pairs={{0,1},{1,0},{2,3},{3,2},{4,5},{5,4},{6,7},{7,6},{8,9},{9,8},{10,11... | collective-permute-start | bytes 663560 | tf_op jit(solution)/shard_map/ppermute | solution.py:451
  19.5 17.9 %collective-permute-start.7 = (f32[432,128]{1,0:T(8,128)S(1)}, f32[432,128]{1,0:T(8,128)S(1)}, u32[]{:S(2)}, u32[]{:S(2)}) collective-permute-start(f32[432,128]{1,0:T(8,128)S(1)} %get-tuple-element.54), channel_id=1, source_target_pairs={{1,2},{2,1},{3,0},{0,3},{5,6},{6,5},{7,4},{4,7},{9,10},{10,9},{11,... | collective-permute-start | bytes 663560 | tf_op jit(solution)/shard_map/ppermute | solution.py:452
  21.4 21.1 %all-to-all-start = ((f32[128,1,128]{2,1,0:T(1,128)}), f32[128,1,128]{2,1,0:T(1,128)S(1)}, u32[]{:S(2)}, u32[]{:S(2)}) async-start(f32[128,1,128]{2,1,0:T(1,128)} %bitcast.13), calls=%async_computation | async-start | bytes 131072 | tf_op jit(solution)/shard_map/all_to_all | solution.py:505
  32.6 3.6 %collective-permute-start.4 = (f32[24,384]{1,0:T(8,128)S(1)}, f32[24,384]{1,0:T(8,128)S(1)}, u32[]{:S(2)}, u32[]{:S(2)}) collective-permute-start(f32[24,384]{1,0:T(8,128)S(1)} %get-tuple-element.51), channel_id=1, source_target_pairs={{0,4},{4,0},{8,12},{12,8},{16,20},{20,16},{24,28},{28,24},{32,36},... | collective-permute-start | bytes 110600 | tf_op jit(solution)/shard_map/ppermute | solution.py:453
  33.7 3.7 %collective-permute-start.5 = (f32[24,384]{1,0:T(8,128)S(1)}, f32[24,384]{1,0:T(8,128)S(1)}, u32[]{:S(2)}, u32[]{:S(2)}) collective-permute-start(f32[24,384]{1,0:T(8,128)S(1)} %get-tuple-element.52), channel_id=1, source_target_pairs={{4,8},{8,4},{12,16},{16,12},{20,24},{24,20},{28,32},{32,28},{36,40... | collective-permute-start | bytes 110600 | tf_op jit(solution)/shard_map/ppermute | solution.py:454

commit v4 on v3

--- a/solution.py
+++ b/solution.py
@@ -432,6 +432,22 @@
         patch_load[c : c + 1, :] = total[:, c * PATCH_DEV : (c + 1) * PATCH_DEV]
 
 
+def held(*arrays):
+    def kernel(*refs):
+        pass
+
+    count = len(arrays)
+    return pl.pallas_call(
+        kernel,
+        out_shape=tuple(f32(*a.shape) for a in arrays),
+        in_specs=[VMEM] * count,
+        out_specs=(VMEM,) * count,
+        input_output_aliases={i: i for i in range(count)},
+        compiler_params=PARAMS,
+        cost_estimate=pl.CostEstimate(flops=4 * 10**6, bytes_accessed=4 * 10**6, transcendentals=0),
+    )(*arrays)
+
+
 def f32(*shape):
     return jax.ShapeDtypeStruct(shape, jnp.float32)
 
@@ -482,7 +498,10 @@
         compiler_params=PARAMS,
     )(*(pltpu.with_memory_space_constraint(x, pltpu.HBM) for x in inputs))
     coefficient = (k1, k2, k3, k4, k5)
-    got = exchanged(*sends)
+    first_c, second_c, first_h, second_h = exchanged(*sends)
+    for _ in range(1):
+        (second_c,) = held(second_c)
+    got = first_c, second_c, first_h, second_h
     rates, pairs, cur, vel = pl.pallas_call(
         middle_kernel,
         out_shape=(f32(*INJECT_SHAPE), jax.ShapeDtypeStruct((FLAT, FLAT), jnp.bfloat16), state, state),

time: 43.3 us -> 43.2 us (level)
  waiting for transfers between devices: 6.6 us -> 4.85 us
  starting transfers between devices: 21.7 us -> 23.3 us
    ppermute x2, starting transfers between devices: 2.38 us -> 4.99 us  [exchanged(): first_c = lax.ppermute(first_c, 'blk', pairs(blks, 0))]
    ppermute x2, waiting for transfers between devices: 2.69 us -> 1.26 us  [exchanged(): second_c = lax.ppermute(second_c, 'blk', pairs(blks, 1))]
    all_to_all x1, starting transfers between devices: 11.2 us -> 9.9 us  [local(): lax.all_to_all(shares, ('blk', 'span'), split_axis=0, concat_axis=0, tile...]
    ppermute x2, starting transfers between devices: 2.36 us -> 3.59 us  [exchanged(): second_c = lax.ppermute(second_c, 'blk', pairs(blks, 1))]
    ppermute x2, starting transfers between devices: 3.63 us -> 2.43 us  [exchanged(): second_h = lax.ppermute(second_h, 'span', pairs(spans, 1))]
    ppermute x2, waiting for transfers between devices: 0.46 us -> 0.01 us  [exchanged(): second_h = lax.ppermute(second_h, 'span', pairs(spans, 1))]
  transfers between devices with their start and end apart: 9 -> 9, of which waited for: 4 -> 3; matrix products, arithmetic and copies ran while one was open for 0% -> 0% of each run, Pallas kernels for 9% -> 9%
where the time goes in v4:
time: 43.2 us; the launch traced here: 43 us
  starting transfers between devices  23.3 us (54%)
  Pallas kernels  14.2 us (33%)
  waiting for transfers between devices  4.85 us (11%)
  between operations  0.69 us (2%)
    all_to_all x1, starting transfers between devices, local(): lax.all_to_all(shares, ('blk', 'span'), split_axis=0, concat_axis=0, tile...  9.9 us
    pallas_call x1, Pallas kernels, local(): pl.pallas_call(first_kernel, out_shape=(flat, flat, face, face, row, row,...  5.55 us
    ppermute x2, starting transfers between devices, exchanged(): first_c = lax.ppermute(first_c, 'blk', pairs(blks, 0))  4.99 us
    pallas_call x1, Pallas kernels, local(): pl.pallas_call(second_kernel, out_shape=(flat, flat, face, face, f32(DEVI...  4.05 us
    ppermute x2, starting transfers between devices, exchanged(): second_c = lax.ppermute(second_c, 'blk', pairs(blks, 1))  3.59 us
    all_to_all x1, waiting for transfers between devices, local(): lax.all_to_all(shares, ('blk', 'span'), split_axis=0, concat_axis=0, tile...  3.45 us
    ppermute x2, starting transfers between devices, exchanged(): first_h = lax.ppermute(first_h, 'span', pairs(spans, 0))  2.43 us
    ppermute x2, starting transfers between devices, exchanged(): second_h = lax.ppermute(second_h, 'span', pairs(spans, 1))  2.43 us
  transfers between devices with their start and end apart: 9, of which 3 were waited for; matrix products, arithmetic and copies ran while one was open for 0% of the time, Pallas kernels for 9%

profile of v4, /device:TPU:1, one launch (start us, length us, event | category | flops | bytes accessed | tf_op | source)
XLA Modules:
  0.0 43.0 jit_solution(198264233203181191)
XLA Ops:
  0.6 5.5 %shard_map.102 = (f32[24,384]{1,0:T(8,128)S(1)}, f32[24,384]{1,0:T(8,128)S(1)}, f32[432,128]{1,0:T(8,128)S(1)}, f32[432,128]{1,0:T(8,128)S(1)}, s32[1,384]{1,0:T...) custom-call(f32[1152,128]{1,0:T(8,128)} %bitcast.20, ...), custom_call_target="tpu_custom_call" | custom-call | tf_op jit(solution)/shard_map/pallas_call | solution.py:489
  6.2 2.1 %collective-permute-start.2 = (f32[432,128]{1,0:T(8,128)S(1)}, f32[432,128]{1,0:T(8,128)S(1)}, u32[]{:S(2)}, u32[]{:S(2)}) collective-permute-start(f32[432,128]{1,0:T(8,128)S(1)} %get-tuple-element.33), channel_id=1, source_target_pairs={{0,1},{1,0},{2,3},{3,2},{4,5},{5,4},{6,7},{7,6},{8,9},{9,8},{10,11... | collective-permute-start | bytes 663560 | tf_op jit(solution)/shard_map/ppermute | solution.py:467
  8.3 1.8 %collective-permute-start.3 = (f32[432,128]{1,0:T(8,128)S(1)}, f32[432,128]{1,0:T(8,128)S(1)}, u32[]{:S(2)}, u32[]{:S(2)}) collective-permute-start(f32[432,128]{1,0:T(8,128)S(1)} %get-tuple-element.34), channel_id=1, source_target_pairs={{1,2},{2,1},{3,0},{0,3},{5,6},{6,5},{7,4},{4,7},{9,10},{10,9},{11,... | collective-permute-start | bytes 663560 | tf_op jit(solution)/shard_map/ppermute | solution.py:468
  10.1 2.8 %collective-permute-start.1 = (f32[24,384]{1,0:T(8,128)S(1)}, f32[24,384]{1,0:T(8,128)S(1)}, u32[]{:S(2)}, u32[]{:S(2)}) collective-permute-start(f32[24,384]{1,0:T(8,128)S(1)} %get-tuple-element.32), channel_id=1, source_target_pairs={{4,8},{8,4},{12,16},{16,12},{20,24},{24,20},{28,32},{32,28},{36,40... | collective-permute-start | bytes 110600 | tf_op jit(solution)/shard_map/ppermute | solution.py:470
  12.9 3.8 %collective-permute-start = (f32[24,384]{1,0:T(8,128)S(1)}, f32[24,384]{1,0:T(8,128)S(1)}, u32[]{:S(2)}, u32[]{:S(2)}) collective-permute-start(f32[24,384]{1,0:T(8,128)S(1)} %get-tuple-element.31), channel_id=1, source_target_pairs={{0,4},{4,0},{8,12},{12,8},{16,20},{20,16},{24,28},{28,24},{32,36},... | collective-permute-start | bytes 110600 | tf_op jit(solution)/shard_map/ppermute | solution.py:469
  16.7 0.7 %shard_map.104 = (f32[4,9,8,128]{3,2,1,0:T(8,128)S(1)}, bf16[384,384]{1,0:T(8,128)(2,1)S(1)}, f32[16,9,8,128]{3,2,1,0:T(8,128)S(1)}, f32[16,9,8,128]{3,2,1,0:T(8,128)S(1)}) custom-call(s32[1,384]{1,0:T(1,128)S(1)} %get-tuple-element.35.match, f32[16,9,8,128]{3,2,1,0:T(8,128)S(1)} %get-tuple-element.36.cur0, ...), custom_call_target="tpu_custom_call", output_to_operand_aliasing={{2}: (1, {}), {3}: (2, {})} | custom-call | flops 3000000 | bytes 4000000 | tf_op jit(solution)/shard_map/pallas_call | solution.py:505
  17.4 0.0 collective-permute-done.1.refs_0_
  17.5 0.1 collective-permute-done.got_first_c
  17.6 0.0 collective-permute-done.2.got_first_h
  17.6 0.0 collective-permute-done.3.got_second_h
  17.6 4.0 %shard_map.105 = (f32[24,384]{1,0:T(8,128)S(1)}, f32[24,384]{1,0:T(8,128)S(1)}, f32[432,128]{1,0:T(8,128)S(1)}, f32[432,128]{1,0:T(8,128)S(1)}, f32[128,128]{1,0...) custom-call(f32[24,384]{1,0:T(8,128)S(1)} %collective-permute-done.g, ...), custom_call_target="tpu_custom_call", output_to_operand_aliasing={{6}: (7, {}), {7}: (8, {})} | custom-call | tf_op jit(solution)/shard_map/pallas_call | solution.py:514
  21.6 0.3 collective-permute-start.6
  22.0 0.6 %collective-permute-start.7 = (f32[432,128]{1,0:T(8,128)S(1)}, f32[432,128]{1,0:T(8,128)S(1)}, u32[]{:S(2)}, u32[]{:S(2)}) collective-permute-start(f32[432,128]{1,0:T(8,128)S(1)} %get-tuple-element.54), channel_id=1, source_target_pairs={{1,2},{2,1},{3,0},{0,3},{5,6},{6,5},{7,4},{4,7},{9,10},{10,9},{11,... | collective-permute-start | bytes 663560 | tf_op jit(solution)/shard_map/ppermute | solution.py:468
  22.6 9.9 %all-to-all-start = ((f32[128,1,128]{2,1,0:T(1,128)}), f32[128,1,128]{2,1,0:T(1,128)S(1)}, u32[]{:S(2)}, u32[]{:S(2)}) async-start(f32[128,1,128]{2,1,0:T(1,128)} %bitcast.13), calls=%async_computation | async-start | bytes 131072 | tf_op jit(solution)/shard_map/all_to_all | solution.py:524
  32.5 1.1 %collective-permute-start.4 = (f32[24,384]{1,0:T(8,128)S(1)}, f32[24,384]{1,0:T(8,128)S(1)}, u32[]{:S(2)}, u32[]{:S(2)}) collective-permute-start(f32[24,384]{1,0:T(8,128)S(1)} %get-tuple-element.51), channel_id=1, source_target_pairs={{0,4},{4,0},{8,12},{12,8},{16,20},{20,16},{24,28},{28,24},{32,36},... | collective-permute-start | bytes 110600 | tf_op jit(solution)/shard_map/ppermute | solution.py:469
  33.6 0.8 %collective-permute-start.5 = (f32[24,384]{1,0:T(8,128)S(1)}, f32[24,384]{1,0:T(8,128)S(1)}, u32[]{:S(2)}, u32[]{:S(2)}) collective-permute-start(f32[24,384]{1,0:T(8,128)S(1)} %get-tuple-element.52), channel_id=1, source_target_pairs={{4,8},{8,4},{12,16},{16,12},{20,24},{24,20},{28,32},{32,28},{36,40... | collective-permute-start | bytes 110600 | tf_op jit(solution)/shard_map/ppermute | solution.py:470
  34.5 1.6 %shard_map.106._ = f32[1152,128]{1,0:T(8,128)} custom-call(f32[16,9,8,128]{3,2,1,0:T(8,128)S(1)} %get-tuple-element.48.cur, f32[16,9,8,128]{3,2,1,0:T(8,128)S(1)} %get-tuple-element.49.vel, f32[4,9,8,128]{3,2,1,0:T(8,128)S(1)} %get-tuple-element.50.inject, f32[16,3,8,128]{3,2,1,0:T(8,128)S(1)} %get-tuple-element.38.refs_0_, ...), custom_call_target="tpu_custom_call" | custom-call | tf_op jit(solution)/shard_map/pallas_call | solution.py:525
  36.1 0.0 collective-permute-done.4.got_first_c
  36.1 1.3 %collective-permute-done.5.got_second_c = f32[24,384]{1,0:T(8,128)S(1)} collective-permute-done((f32[24,384]{1,0:T(8,128)S(1)}, f32[24,384]{1,0:T(8,128)S(1)}, u32[]{:S(2)}, u32[]{:S(2)}) %collective-permute-start.5) | collective-permute-done | bytes 36896 | tf_op jit(solution)/shard_map/ppermute | solution.py:470
  37.4 0.0 collective-permute-done.6.got_first_h
  37.4 0.0 collective-permute-done.7.got_second_h
  37.4 1.5 %shard_map.107 = (f32[576,24]{1,0:T(8,128)}, f32[864,128]{1,0:T(8,128)}) custom-call(f32[24,384]{1,0:T(8,128)S(1)} %collective-permute-done.4.got_first_c, f32[24,384]{1,0:T(8,128)S(1)} %collective-permute-done.5.got_second_c, f32[432,128]{1,0:T(8,128)S(1)} %collective-permute-done.6.got_first_h, f32[432,128]{1,0:T(8,128)S(1)} %collective-permute-done.7.got_second_h, ...), custom_call_target="tpu_custom_call" | custom-call | tf_op jit(solution)/shard_map/pallas_call | solution.py:533
  38.9 3.4 %all-to-all-done = f32[128,1,128]{2,1,0:T(1,128)S(1)} async-done(((f32[128,1,128]{2,1,0:T(1,128)}), f32[128,1,128]{2,1,0:T(1,128)S(1)}, u32[]{:S(2)}, u32[]{:S(2)}) %all-to-all-start) | async-done | bytes 65568 | tf_op jit(solution)/shard_map/all_to_all | solution.py:524
  42.4 0.7 %shard_map.108 = f32[3,32]{1,0:T(4,128)} custom-call(f32[128,128]{1,0:T(8,128)S(1)} %bitcast.18, f32[576,24]{1,0:T(8,128)} %get-tuple-element.55._), custom_call_target="tpu_custom_call" | custom-call | tf_op jit(solution)/shard_map/pallas_call | solution.py:541
  (1 shorter events, 0.0 us)
Async XLA Ops:
  6.2 11.4 %collective-permute-start.2 = (f32[432,128]{1,0:T(8,128)S(1)}, f32[432,128]{1,0:T(8,128)S(1)}, u32[]{:S(2)}, u32[]{:S(2)}) collective-permute-start(f32[432,128]{1,0:T(8,128)S(1)} %get-tuple-element.33), channel_id=1, source_target_pairs={{0,1},{1,0},{2,3},{3,2},{4,5},{5,4},{6,7},{7,6},{8,9},{9,8},{10,11... | collective-permute-start | bytes 663560 | tf_op jit(solution)/shard_map/ppermute | solution.py:467
  8.3 9.3 %collective-permute-start.3 = (f32[432,128]{1,0:T(8,128)S(1)}, f32[432,128]{1,0:T(8,128)S(1)}, u32[]{:S(2)}, u32[]{:S(2)}) collective-permute-start(f32[432,128]{1,0:T(8,128)S(1)} %get-tuple-element.34), channel_id=1, source_target_pairs={{1,2},{2,1},{3,0},{0,3},{5,6},{6,5},{7,4},{4,7},{9,10},{10,9},{11,... | collective-permute-start | bytes 663560 | tf_op jit(solution)/shard_map/ppermute | solution.py:468
  10.1 7.3 %collective-permute-start.1 = (f32[24,384]{1,0:T(8,128)S(1)}, f32[24,384]{1,0:T(8,128)S(1)}, u32[]{:S(2)}, u32[]{:S(2)}) collective-permute-start(f32[24,384]{1,0:T(8,128)S(1)} %get-tuple-element.32), channel_id=1, source_target_pairs={{4,8},{8,4},{12,16},{16,12},{20,24},{24,20},{28,32},{32,28},{36,40... | collective-permute-start | bytes 110600 | tf_op jit(solution)/shard_map/ppermute | solution.py:470
  12.9 4.7 %collective-permute-start = (f32[24,384]{1,0:T(8,128)S(1)}, f32[24,384]{1,0:T(8,128)S(1)}, u32[]{:S(2)}, u32[]{:S(2)}) collective-permute-start(f32[24,384]{1,0:T(8,128)S(1)} %get-tuple-element.31), channel_id=1, source_target_pairs={{0,4},{4,0},{8,12},{12,8},{16,20},{20,16},{24,28},{28,24},{32,36},... | collective-permute-start | bytes 110600 | tf_op jit(solution)/shard_map/ppermute | solution.py:469
  21.6 15.7 %collective-permute-start.6 = (f32[432,128]{1,0:T(8,128)S(1)}, f32[432,128]{1,0:T(8,128)S(1)}, u32[]{:S(2)}, u32[]{:S(2)}) collective-permute-start(f32[432,128]{1,0:T(8,128)S(1)} %get-tuple-element.53), channel_id=1, source_target_pairs={{0,1},{1,0},{2,3},{3,2},{4,5},{5,4},{6,7},{7,6},{8,9},{9,8},{10,11... | collective-permute-start | bytes 663560 | tf_op jit(solution)/shard_map/ppermute | solution.py:467
  22.0 15.4 %collective-permute-start.7 = (f32[432,128]{1,0:T(8,128)S(1)}, f32[432,128]{1,0:T(8,128)S(1)}, u32[]{:S(2)}, u32[]{:S(2)}) collective-permute-start(f32[432,128]{1,0:T(8,128)S(1)} %get-tuple-element.54), channel_id=1, source_target_pairs={{1,2},{2,1},{3,0},{0,3},{5,6},{6,5},{7,4},{4,7},{9,10},{10,9},{11,... | collective-permute-start | bytes 663560 | tf_op jit(solution)/shard_map/ppermute | solution.py:468
  22.6 19.8 %all-to-all-start = ((f32[128,1,128]{2,1,0:T(1,128)}), f32[128,1,128]{2,1,0:T(1,128)S(1)}, u32[]{:S(2)}, u32[]{:S(2)}) async-start(f32[128,1,128]{2,1,0:T(1,128)} %bitcast.13), calls=%async_computation | async-start | bytes 131072 | tf_op jit(solution)/shard_map/all_to_all | solution.py:524
  32.5 3.6 %collective-permute-start.4 = (f32[24,384]{1,0:T(8,128)S(1)}, f32[24,384]{1,0:T(8,128)S(1)}, u32[]{:S(2)}, u32[]{:S(2)}) collective-permute-start(f32[24,384]{1,0:T(8,128)S(1)} %get-tuple-element.51), channel_id=1, source_target_pairs={{0,4},{4,0},{8,12},{12,8},{16,20},{20,16},{24,28},{28,24},{32,36},... | collective-permute-start | bytes 110600 | tf_op jit(solution)/shard_map/ppermute | solution.py:469
  33.6 3.7 %collective-permute-start.5 = (f32[24,384]{1,0:T(8,128)S(1)}, f32[24,384]{1,0:T(8,128)S(1)}, u32[]{:S(2)}, u32[]{:S(2)}) collective-permute-start(f32[24,384]{1,0:T(8,128)S(1)} %get-tuple-element.52), channel_id=1, source_target_pairs={{4,8},{8,4},{12,16},{16,12},{20,24},{24,20},{28,32},{32,28},{36,40... | collective-permute-start | bytes 110600 | tf_op jit(solution)/shard_map/ppermute | solution.py:470
